TPU v7x, 32 devices: a whole 2x2x4 slice. The times are simulated.
32 devices in a mesh: dp: 16 (over z, x, core), tensor: 2 (over y).
Axes of the slice: x: 2, y: 2, z: 4, core: 2. Of those that a mesh axis runs over, the one named last changes fastest.
Arguments:
- tokens: bfloat16 [32768, 768], P(('dp', 'tensor')), may hold values from -6 to 6
- segment: int32 [32768], P('dp'), may hold values from 0 to 16, as said below
- weight_qkv: bfloat16 [3, 768, 768], P(None, 'dp', 'tensor'), may hold values from -0.3125 to 0.3125
- weight_out: bfloat16 [768, 768], P('tensor', 'dp'), may hold values from -0.625 to 0.625
- weight_in: bfloat16 [768, 3072], P('dp', 'tensor'), may hold values from -0.21875 to 0.21875
- weight_down: bfloat16 [3072, 768], P('tensor', 'dp'), may hold values from -0.15625 to 0.15625
- gain_one: bfloat16 [768], P('dp'), may hold values from 0.5 to 1.5
- shift_one: bfloat16 [768], P('dp'), may hold values from -3 to 3
- gain_two: bfloat16 [768], P('dp'), may hold values from 0.5 to 1.5
- shift_two: bfloat16 [768], P('dp'), may hold values from -3 to 3
- cotangent: bfloat16 [32768, 768], P(('dp', 'tensor')), may hold values from -6 to 6
Outputs:
- output: bfloat16 [32768, 768], P(('dp', 'tensor'))
- input_grad: bfloat16 [32768, 768], P(('dp', 'tensor'))
- grad_weight_qkv: float32 [3, 768, 768], P(None, 'dp', 'tensor')
- grad_weight_out: float32 [768, 768], P('tensor', 'dp')
- grad_weight_in: float32 [768, 3072], P('dp', 'tensor')
- grad_weight_down: float32 [3072, 768], P('tensor', 'dp')
- grad_gain_one: float32 [768], P('dp')
- grad_shift_one: float32 [768], P('dp')
- grad_gain_two: float32 [768], P('dp')
- grad_shift_two: float32 [768], P('dp')
Inputs may be any that keep to these rules, and one draw needn't show every extreme that they name: `segment`: segment numbers start at 0 in each sequence of 512 consecutive tokens and rise by one at each document's first token; each document has 20 to 200 tokens except the last of a sequence, which may be cut shorter; every sequence holds a document of exactly 200 tokens.
All inputs are finite; a program needn't handle non-finite values.
Results may differ from a plain program's by a relative error of at most 0.02.
Values may be sent and summed in bfloat16 or wider, within the bound.
No kernel may reach another device: no remote copies, remote signals or barrier semaphores. Data moves between devices by JAX's collectives and lax.ppermute only.
A program may use at most 192 MiB of HBM per device.

v0:
```python
import functools

import jax
import jax.numpy as jnp
from jax import lax
from jax.experimental import pallas as pl
from jax.experimental.pallas import tpu as pltpu
from jax.sharding import PartitionSpec as P

HDIM = 64
SEQ = 512
LANES = 128
EDGE = 256
BLOCK = 256
CHUNK = 256
VMEM = 56 * 1024 * 1024
epsilon = 1e-05
SMALL = pl.CostEstimate(flops=100_000_000, bytes_accessed=100_000, transcendentals=0)


def low(value):
    return value.astype(jnp.bfloat16)


AXES = ("dp", "tensor")
ZS = 4


def place(z, x, c, y):
    return ((z * 2 + x) * 2 + c) * 2 + y


def pairs(move):
    found = []
    for z in range(ZS):
        for x in range(2):
            for c in range(2):
                for y in range(2):
                    found.append((place(z, x, c, y), place(*move(z, x, c, y))))
    return found


TO_CORE = pairs(lambda z, x, c, y: (z, x, 1 - c, y))
TO_NEAR = pairs(lambda z, x, c, y: (z, x, c, 1 - y) if c else (z, 1 - x, c, y))
TO_FAR = pairs(lambda z, x, c, y: (z, 1 - x, c, y) if c else (z, x, c, 1 - y))
TO_DEPTH = [pairs(lambda z, x, c, y: ((z - k) % ZS, x, c, y)) for k in range(ZS)]


def coords():
    d = lax.axis_index("dp")
    y = lax.axis_index("tensor")
    return d // 4, (d // 2) % 2, d % 2, y


def send(value, route):
    return lax.ppermute(value, AXES, route)


def in_order(own, other, at):
    return jnp.where(at == 0, jnp.stack([own, other]), jnp.stack([other, own]))


def tuned():
    return lax.axis_size("dp") == 16 and lax.axis_size("tensor") == 2


def sync(*values):
    found = lax.optimization_barrier([value.value if isinstance(value, Flow) else value for value in values])
    for value, new in zip(values, found):
        if isinstance(value, Flow):
            value.value = new
    found = [new for value, new in zip(values, found) if not isinstance(value, Flow)]
    return found[0] if len(found) == 1 else found


def hold(pieces, *values):
    if not isinstance(pieces, list):
        return pieces
    return [*pieces[:-1], sync(pieces[-1], *values)]


class Flow:
    def __init__(self, steps):
        self.steps = steps
        self.value = next(steps)

    def go(self, count=1):
        for _ in range(count):
            self.value = self.steps.send(self.value)
        return self.value


def gather_steps(left, right):
    if not tuned():
        for _ in range(10):
            left = yield left
        full = lax.all_gather(jnp.concatenate([left, right], axis=1), ("tensor", "dp"), axis=0, tiled=True)
        full = full.reshape(2, ZS, 2, -1, full.shape[1])
        left, right = jnp.split(full, 2, axis=4)
        left = jnp.transpose(left, (0, 2, 1, 3, 4))
        right = jnp.transpose(right, (2, 0, 1, 3, 4))
        yield left, right, jnp.zeros((1,), jnp.int32)
        return
    z, x, c, y = coords()
    first = c == 0
    own = yield jnp.where(first, right, left)
    got = yield send(own, TO_CORE)
    mine = jnp.where(first, jnp.concatenate([left, got]), jnp.concatenate([got, right]))
    mine = yield mine
    got = yield [send(mine, TO_DEPTH[k]) for k in (1, 2, 3)]
    column = jnp.stack([mine, *got, mine, *got[:2]])
    column = yield lax.dynamic_slice_in_dim(column, (ZS - z) % ZS, ZS, 0)
    near = yield send(column, TO_NEAR)
    plane = yield in_order(column, near, jnp.where(first, x, y))
    far = yield send(plane, TO_FAR)
    whole = yield in_order(plane, far, jnp.where(first, y, x))
    sibling = yield send(whole, TO_CORE)
    yield whole, sibling, c.astype(jnp.int32).reshape(1)


def add(a, b):
    return a.astype(jnp.float32) + b.astype(jnp.float32)


def pick(value, at):
    return lax.dynamic_index_in_dim(value, at, 0, keepdims=False)


def core_side():
    return coords()[2].astype(jnp.int32) if tuned() else jnp.int32(0)


def place_of(own):
    _, x, _, y = coords()
    side = core_side() if own else 1 - core_side()
    at = jnp.where(side == 0, y, x) if tuned() else 0 * y
    return jnp.stack([side, at.astype(jnp.int32)])


def exchange(value):
    return send(value, TO_CORE) if tuned() else jnp.zeros_like(value)


def scatter_steps(part):
    if not tuned():
        left, right = [jnp.stack(part(own)) for own in (True, False)]
        left = yield left
        for _ in range(7):
            left = yield left
        left = jnp.transpose(left, (0, 2, 1, 3, 4))
        right = jnp.transpose(right, (1, 2, 0, 3, 4))
        full = jnp.concatenate([left, right], axis=4)
        full = lax.psum_scatter(
            full.reshape(-1, full.shape[4]), ("tensor", "dp"), scatter_dimension=0, tiled=True
        )
        full = lax.optimization_barrier(full).astype(jnp.float32)
        yield tuple(jnp.split(full, 2, axis=1))
        return
    z, x, c, y = coords()
    first = c == 0
    stay, away = part(True)
    away = yield away
    got = yield send(away, TO_FAR)
    total = low(add(stay, got))
    at = jnp.where(first, x, y)
    away = yield pick(total, 1 - at)
    got = yield send(away, TO_NEAR)
    total = low(add(pick(total, at), got))
    away = yield [pick(total, (z - k) % ZS) for k in (1, 2, 3)]
    got = yield [send(piece, TO_DEPTH[k + 1]) for k, piece in enumerate(away)]
    total = pick(total, z).astype(jnp.float32)
    for piece in got:
        total = total + piece.astype(jnp.float32)
    total = total.reshape(2, -1, total.shape[1])
    away = yield pick(total, 1 - c)
    got = yield send(away, TO_CORE)
    keep = pick(total, c)
    yield jnp.where(first, keep, got), jnp.where(first, got, keep)


def dot_nn(left, right):
    return lax.dot_general(left, right, (((1,), (0,)), ((), ())), preferred_element_type=jnp.float32)


def dot_nt(left, right):
    return lax.dot_general(left, right, (((1,), (1,)), ((), ())), preferred_element_type=jnp.float32)


def flip(value):
    return jnp.swapaxes(value, 0, 1)


def load_set(side_ref, mine_ref, other_ref, left, right, sems, only=None):
    count = mine_ref.shape[3]

    def start(left_ref, right_ref):
        for y in range(2) if only is None else (only,):
            at = y if only is None else 0
            for x in range(2):
                for z in range(ZS):
                    cut = pl.ds((z * 2 + x) * count, count)
                    pltpu.make_async_copy(left_ref.at[y, x, z], left.at[at, cut], sems.at[0]).start()
                    pltpu.make_async_copy(right_ref.at[x, y, z], right.at[at, cut], sems.at[1]).start()

    @pl.when(side_ref[0] == 0)
    def _():
        start(mine_ref, other_ref)

    @pl.when(side_ref[0] != 0)
    def _():
        start(other_ref, mine_ref)


def load_halves(side_ref, mine_ref, other_ref, mine, other, sems):
    count = mine_ref.shape[3]

    def start(flipped):
        for y in range(2):
            for x in range(2):
                for z in range(ZS):
                    cut = pl.ds((z * 2 + x) * count, count)
                    for source, target, sem, turned in (
                        (mine_ref, mine, sems.at[0], flipped), (other_ref, other, sems.at[1], not flipped),
                    ):
                        block = source.at[x, y, z] if turned else source.at[y, x, z]
                        pltpu.make_async_copy(block, target.at[y, cut], sem).start()

    @pl.when(side_ref[0] == 0)
    def _():
        start(False)

    @pl.when(side_ref[0] != 0)
    def _():
        start(True)


def wait_set(left, right, sems):
    pltpu.make_async_copy(left, left, sems.at[0]).wait()
    pltpu.make_async_copy(right, right, sems.at[1]).wait()


def set_scratch(weights, count=2):
    width, cols = 8 * weights[0].shape[3], weights[0].shape[4]
    buffer = pltpu.VMEM((count, width, cols), jnp.bfloat16)
    return [buffer, buffer, pltpu.SemaphoreType.DMA((2,))]


def set_specs():
    return [
        pl.BlockSpec(memory_space=pltpu.SMEM),
        pl.BlockSpec(memory_space=pl.ANY),
        pl.BlockSpec(memory_space=pl.ANY),
    ]


def set_args(weights):
    return weights[2], weights[0], weights[1]


def params():
    return pltpu.CompilerParams(vmem_limit_bytes=VMEM)


def pair_cols(left, right, at):
    start = at * LANES
    width = left.shape[-1]
    if start < width:
        return left[:, start : start + LANES]
    return right[:, start - width : start - width + LANES]


def by_head(value):
    lane = lax.broadcasted_iota(jnp.int32, value.shape, 1)
    blank = jnp.zeros_like(value)
    return jnp.concatenate([jnp.where(lane < HDIM, value, blank), jnp.where(lane < HDIM, blank, value)], axis=0)


def own_heads(value):
    return jnp.concatenate([value[:HDIM, :SEQ], value[HDIM:, SEQ:]], axis=0)


def attend_kernel(t, carried, side_ref, mine_ref, other_ref, x_ref, row_ref, col_ref, *refs):
    pa_ref, pb_ref, e_ref, att_ref, flat_ref, inv_ref, bias_ref, a_ref, b_ref, sems = refs[carried:]
    pairs = flat_ref.shape[2] // LANES
    load_set(side_ref, mine_ref, other_ref, a_ref, b_ref, sems, t)
    wait_set(a_ref, b_ref, sems)

    x = x_ref[...]
    pa_ref[0] = low(dot_nn(x, a_ref[0]))
    pb_ref[0] = low(dot_nn(x, b_ref[0, :, : pb_ref.shape[2]]))
    bias = jnp.where(col_ref[0, :, :1] == row_ref[0], 0.0, -1e30)
    bias_ref[:, :SEQ] = bias
    bias_ref[:, SEQ:] = bias
    left, right = pa_ref[0], pb_ref[0]
    for p in range(pairs):
        queries = by_head(low(pair_cols(left, right, p).astype(jnp.float32) * HDIM**-0.5))
        key_rows = pair_cols(left, right, pairs + p)
        values_flat = flip(pair_cols(left, right, 2 * pairs + p))
        scores = dot_nt(key_rows, queries) + bias_ref[...]
        weights = jnp.exp(scores - jnp.max(scores, axis=0, keepdims=True))
        inverse = 1.0 / jnp.sum(weights, axis=0, keepdims=True)
        weights = low(weights)
        e_ref[0, p] = weights
        inv_ref[0, p : p + 1, :] = inverse
        flat = low(own_heads(dot_nn(values_flat, weights) * inverse))
        flat_ref[0, 0, p * LANES : (p + 1) * LANES, :] = flat
        at = p * LANES
        att_ref[at // EDGE, :, at % EDGE : at % EDGE + LANES] = flip(flat)
    at = pairs * LANES
    att_ref[at // EDGE, :, at % EDGE :] = jnp.zeros((SEQ, LANES), jnp.bfloat16)


def attend(tokens, weights, numbers, t, s, carry=()):
    rows, width = tokens.shape
    seqs = rows // SEQ
    cols = weights[0].shape[4]
    wide = (2 * cols - LANES) // 3
    pairs = wide // LANES
    used = cols - LANES
    bf = jnp.bfloat16
    at = lambda *index: (lambda i: index)
    return pl.pallas_call(
        functools.partial(attend_kernel, t, len(carry)),
        grid=(1,),
        in_specs=set_specs() + [
            pl.BlockSpec((SEQ, width), at(s, 0)),
            pl.BlockSpec((1, 1, SEQ), at(s, 0, 0)),
            pl.BlockSpec((1, SEQ, LANES), at(s, 0, 0)),
        ] + [pl.BlockSpec(memory_space=pl.ANY)] * len(carry),
        out_specs=[
            pl.BlockSpec((1, SEQ, cols), at(0, s, 0)),
            pl.BlockSpec((1, SEQ, used), at(0, s, 0)),
            pl.BlockSpec((1, pairs, SEQ, 2 * SEQ), at(s, 0, 0, 0)),
            pl.BlockSpec((2, SEQ, EDGE), at(0, s, 0)),
            pl.BlockSpec((1, 1, wide, SEQ), at(0, s, 0, 0)),
            pl.BlockSpec((1, pairs, 2 * SEQ), at(s, 0, 0)),
        ],
        out_shape=[
            jax.ShapeDtypeStruct((1, rows, cols), bf),
            jax.ShapeDtypeStruct((1, rows, used), bf),
            jax.ShapeDtypeStruct((seqs, pairs, SEQ, 2 * SEQ), bf),
            jax.ShapeDtypeStruct((2, rows, EDGE), bf),
            jax.ShapeDtypeStruct((1, seqs, wide, SEQ), bf),
            jax.ShapeDtypeStruct((seqs, pairs, 2 * SEQ), jnp.float32),
        ],
        input_output_aliases={6 + i: i for i in range(len(carry))},
        scratch_shapes=[pltpu.VMEM((SEQ, 2 * SEQ), jnp.float32)] + set_scratch(weights, 1),
        compiler_params=params(),
        cost_estimate=SMALL,
        name="attend",
    )(*set_args(weights), tokens, *numbers, *carry)


def attend_back_kernel(
    t, side_ref, mine_ref, other_ref, g_ref, pa_ref, pb_ref, e_ref, flat_ref, inv_ref,
    dm_ref, do_ref, w_ref, gt_ref, sem,
):
    wide = flat_ref.shape[2]
    pairs = wide // LANES
    count = mine_ref.shape[3]

    @pl.when(pl.program_id(0) == 0)
    def _():
        def start(left_ref, right_ref):
            cols = pl.ds(0, EDGE)
            for x in range(2):
                for z in range(ZS):
                    cut = pl.ds((z * 2 + x) * count, count)
                    pltpu.make_async_copy(left_ref.at[t, x, z, :, cols], w_ref.at[0, cut], sem).start()
                    pltpu.make_async_copy(right_ref.at[x, t, z, :, cols], w_ref.at[1, cut], sem).start()

        @pl.when(side_ref[0] == 0)
        def _():
            start(mine_ref, other_ref)

        @pl.when(side_ref[0] != 0)
        def _():
            start(other_ref, mine_ref)

        pltpu.make_async_copy(w_ref, w_ref, sem).wait()

    for side in range(2):
        size = min(EDGE, wide - side * EDGE)
        gt_ref[side * EDGE : side * EDGE + size] = flip(low(dot_nn(g_ref[...], w_ref[side, :, :size])))
    left, right = pa_ref[0], pb_ref[0]
    found = {}
    blank = jnp.zeros((HDIM, SEQ), jnp.bfloat16)
    for p in range(pairs):
        queries = by_head(pair_cols(left, right, p))
        keys_flat = flip(pair_cols(left, right, pairs + p))
        value_rows = pair_cols(left, right, 2 * pairs + p)
        flat = flat_ref[0, 0, p * LANES : (p + 1) * LANES, :].astype(jnp.float32)
        scaled, centre = [], []
        for half in range(2):
            rows = slice(half * HDIM, (half + 1) * HDIM)
            grads = gt_ref[p * LANES + half * HDIM : p * LANES + (half + 1) * HDIM, :].astype(jnp.float32)
            scaled.append(low(grads * inv_ref[0, p : p + 1, half * SEQ : (half + 1) * SEQ]))
            centre.append(jnp.sum(scaled[half].astype(jnp.float32) * flat[rows], axis=0, keepdims=True))
        grads = jnp.concatenate(
            [jnp.concatenate([scaled[0], blank], axis=0), jnp.concatenate([blank, scaled[1]], axis=0)], axis=1
        )
        weights = e_ref[0, p]
        grad_weights = dot_nn(value_rows, grads) - jnp.concatenate(centre, axis=1)
        grad_scores = low(weights.astype(jnp.float32) * grad_weights)
        found[p] = flip(low(own_heads(dot_nn(keys_flat, grad_scores)) * HDIM**-0.5))
        found[pairs + p] = low(dot_nn(grad_scores, queries) * HDIM**-0.5)
        found[2 * pairs + p] = low(dot_nn(weights, flip(grads)))
    found[3 * pairs] = jnp.zeros((SEQ, LANES), jnp.bfloat16)
    count = (3 * pairs + 1) // 2
    for at in range(count):
        cut = slice(at * LANES, (at + 1) * LANES)
        dm_ref[:, cut] = jnp.where(side_ref[0] == 0, found[at], found[at + count])
        do_ref[:, cut] = jnp.where(side_ref[0] == 0, found[at + count], found[at])


def attend_back(grad_branch, weights, kept, t):
    pa, pb, e, _, flat, inv = kept
    rows, width = grad_branch.shape
    seqs = rows // SEQ
    cols, used = pa.shape[2], pb.shape[2]
    wide = flat.shape[2]
    bf = jnp.bfloat16
    return pl.pallas_call(
        functools.partial(attend_back_kernel, t),
        grid=(seqs,),
        in_specs=set_specs() + [
            pl.BlockSpec((SEQ, width), lambda s: (s, 0)),
            pl.BlockSpec((1, SEQ, cols), lambda s: (0, s, 0)),
            pl.BlockSpec((1, SEQ, used), lambda s: (0, s, 0)),
            pl.BlockSpec((1,) + e.shape[1:], lambda s: (s, 0, 0, 0)),
            pl.BlockSpec((1, 1, wide, SEQ), lambda s: (0, s, 0, 0)),
            pl.BlockSpec((1,) + inv.shape[1:], lambda s: (s, 0, 0)),
        ],
        out_specs=[pl.BlockSpec((SEQ, cols), lambda s: (s, 0))] * 2,
        out_shape=[jax.ShapeDtypeStruct((rows, cols), bf)] * 2,
        scratch_shapes=[
            pltpu.VMEM((2, width, EDGE), bf),
            pltpu.VMEM((wide, SEQ), bf),
            pltpu.SemaphoreType.DMA,
        ],
        compiler_params=params(),
        cost_estimate=SMALL,
        name="attend_back",
    )(*set_args(weights), grad_branch, pa, pb, e, flat, inv)


def gelu_parts(v):
    below = 0.5 + 0.5 * lax.erf(v * 0.5**0.5)
    bell = jnp.exp(-0.5 * (v * v))
    return v * below, below + (0.3989422804014327 * v) * bell


def row_norm(value):
    centered = value - jnp.mean(value, axis=-1, keepdims=True)
    inverse = lax.rsqrt(jnp.mean(centered * centered, axis=-1, keepdims=True) + epsilon)
    return centered * inverse, inverse


def row_norm_back(grad_scaled, scaled, inverse):
    centered = grad_scaled - jnp.mean(grad_scaled, axis=-1, keepdims=True)
    return inverse * (centered - scaled * jnp.mean(grad_scaled * scaled, axis=-1, keepdims=True))


def widen_kernel(
    side_ref, mine_ref, other_ref, x_ref, u_ref, v_ref, n_ref,
    sum_ref, tok_ref, low_ref, hm_ref, ho_ref, sm_ref, so_ref, mine, other, sems,
):
    @pl.when(pl.program_id(0) == 0)
    def _():
        load_halves(side_ref, mine_ref, other_ref, mine, other, sems)
        wait_set(mine, other, sems)

    tok_ref[...] = flip(x_ref[...])
    total = x_ref[...].astype(jnp.float32)
    for t, ref in enumerate((u_ref, v_ref)):
        near = jnp.where(side_ref[0] == 0, ref[0], ref[1])
        away = jnp.where(side_ref[0] == 0, ref[1], ref[0])
        total = total + dot_nt(near, mine[t, :, :EDGE]) + dot_nt(away, other[t, :, :EDGE])
    sum_ref[...] = total
    scaled, _ = row_norm(total)
    x = low(scaled * n_ref[0:1, :] + n_ref[1:2, :])
    low_ref[...] = flip(x)
    half = mine.shape[2] - EDGE
    for t in range(2):
        for ref, hid_ref, slope_ref in ((mine, hm_ref, sm_ref), (other, ho_ref, so_ref)):
            for start in range(0, half, CHUNK):
                cut = slice(t * half + start, t * half + start + CHUNK)
                value, slope = gelu_parts(dot_nn(x, ref[t, :, EDGE + start : EDGE + start + CHUNK]))
                hid_ref[:, cut] = low(value)
                slope_ref[:, cut] = low(slope)


def widen(tokens, attended, weights, norms):
    rows, width = tokens.shape
    span = 2 * (weights[0].shape[4] - EDGE)
    bf = jnp.bfloat16
    by_row = lambda n: pl.BlockSpec((BLOCK, n), lambda r: (r, 0))
    full = lambda a: pl.BlockSpec(a.shape, lambda r: (0, 0))
    side = pl.BlockSpec((2, BLOCK, EDGE), lambda r: (0, r, 0))
    return pl.pallas_call(
        widen_kernel,
        grid=(rows // BLOCK,),
        in_specs=set_specs() + [by_row(width), side, side, full(norms)],
        out_specs=[by_row(width)] + [pl.BlockSpec((width, BLOCK), lambda r: (0, r))] * 2 + [by_row(span)] * 4,
        out_shape=[
            jax.ShapeDtypeStruct((rows, width), jnp.float32),
            jax.ShapeDtypeStruct((width, rows), bf),
            jax.ShapeDtypeStruct((width, rows), bf),
        ] + [jax.ShapeDtypeStruct((rows, span), bf)] * 4,
        scratch_shapes=set_scratch(weights),
        compiler_params=params(),
        cost_estimate=SMALL,
        name="widen",
    )(*set_args(weights), tokens, *attended, norms)


def middle_kernel(
    side_ref, mine_ref, other_ref, side_two_ref, mine_two_ref, other_two_ref,
    sum_ref, hm_ref, ho_ref, sm_ref, so_ref, n_ref, cot_ref,
    out_ref, gs_ref, gm_ref, go_ref, res_ref, gb_ref, gbt_ref, flat_ref,
    mine, other, sems, win_mine, win_other, win_sems, stat_ref,
):
    @pl.when(pl.program_id(0) == 0)
    def _():
        load_halves(side_ref, mine_ref, other_ref, mine, other, sems)
        load_halves(side_two_ref, mine_two_ref, other_two_ref, win_mine, win_other, win_sems)
        wait_set(mine, other, sems)

    gain_one, shift_one = n_ref[0:1, :], n_ref[1:2, :]
    gain_two, shift_two = n_ref[2:3, :], n_ref[3:4, :]
    scaled_one, inverse_one = row_norm(sum_ref[...])
    value = scaled_one * gain_one + shift_one
    half = mine.shape[2]
    for t in range(2):
        for ref, hid_ref in ((mine, hm_ref), (other, ho_ref)):
            value = value + dot_nt(hid_ref[:, t * half : (t + 1) * half], ref[t])
    scaled_two, inverse_two = row_norm(value)
    out_ref[...] = low(scaled_two * gain_two + shift_two)
    cotangent = cot_ref[...].astype(jnp.float32)
    grad_two = row_norm_back(cotangent * gain_two, scaled_two, inverse_two)
    grad_second = low(grad_two)
    gs_ref[...] = flip(grad_second)
    for t in range(2):
        for ref, slope_ref, gi_ref in ((mine, sm_ref, gm_ref), (other, so_ref, go_ref)):
            for start in range(0, half, CHUNK):
                cut = slice(t * half + start, t * half + start + CHUNK)
                grad_hidden = dot_nn(grad_second, ref[t, :, start : start + CHUNK])
                gi_ref[:, cut] = low(grad_hidden * slope_ref[:, cut].astype(jnp.float32))

    @pl.when(pl.program_id(0) == 0)
    def _():
        wait_set(win_mine, win_other, win_sems)
        stat_ref[...] = jnp.zeros_like(stat_ref)

    grad_first = grad_two
    for t in range(2):
        for ref, gi_ref in ((win_mine, gm_ref), (win_other, go_ref)):
            grad_first = grad_first + dot_nt(gi_ref[:, t * half : (t + 1) * half], ref[t, :, EDGE:])
    grad_one = row_norm_back(grad_first * gain_one, scaled_one, inverse_one)
    res_ref[...] = grad_one
    gb_ref[...] = low(grad_one)
    gbt_ref[...] = flip(low(grad_one))
    for row, value in enumerate((grad_first * scaled_one, grad_first, cotangent * scaled_two, cotangent)):
        stat_ref[row : row + 1, :] += jnp.sum(value, axis=0, keepdims=True)

    @pl.when(pl.program_id(0) == pl.num_programs(0) - 1)
    def _():
        flat_ref[...] = flip(stat_ref[...])


def middle(total, hidden, slope, weights_down, weights_in, norms, cotangent):
    rows, width = total.shape
    span = hidden[0].shape[1]
    bf = jnp.bfloat16
    by_row = lambda n: pl.BlockSpec((BLOCK, n), lambda r: (r, 0))
    by_col = pl.BlockSpec((width, BLOCK), lambda r: (0, r))
    full = lambda a: pl.BlockSpec(a.shape, lambda r: (0, 0))
    return pl.pallas_call(
        middle_kernel,
        grid=(rows // BLOCK,),
        in_specs=set_specs() * 2 + [by_row(width)] + [by_row(span)] * 4 + [full(norms), by_row(width)],
        out_specs=[
            by_row(width), by_col, by_row(span), by_row(span), by_row(width), by_row(width), by_col,
            pl.BlockSpec((width, LANES), lambda r: (0, 0)),
        ],
        out_shape=[
            jax.ShapeDtypeStruct((rows, width), bf),
            jax.ShapeDtypeStruct((width, rows), bf),
            jax.ShapeDtypeStruct((rows, span), bf),
            jax.ShapeDtypeStruct((rows, span), bf),
            jax.ShapeDtypeStruct((rows, width), jnp.float32),
            jax.ShapeDtypeStruct((rows, width), bf),
            jax.ShapeDtypeStruct((width, rows), bf),
            jax.ShapeDtypeStruct((width, LANES), jnp.float32),
        ],
        scratch_shapes=set_scratch(weights_down) + set_scratch(weights_in) + [pltpu.VMEM((LANES, width), jnp.float32)],
        compiler_params=params(),
        cost_estimate=SMALL,
        name="middle",
    )(*set_args(weights_down), *set_args(weights_in), total, *hidden, *slope, norms, cotangent)


def store_rows(place_ref, t, refs, value, cut):
    stay_ref, away_ref = refs
    count = stay_ref.shape[2]
    for x in range(2):
        a = jnp.where(place_ref[0] == 0, t, x)
        b = jnp.where(place_ref[0] == 0, x, t)
        for z in range(ZS):
            start = (z * 2 + x) * count
            piece = low(value[start : start + count])

            @pl.when(a == place_ref[1])
            def _():
                stay_ref[b, z, :, cut] = piece

            @pl.when(a != place_ref[1])
            def _():
                away_ref[b, z, :, cut] = piece


def weigh_kernel(jobs, place_ref, stats_ref, stats_got_ref, *refs):
    refs = list(refs)
    sources = [refs.pop(0) for _ in range(6 * len(jobs))]
    outs = refs.pop(0), refs.pop(0)
    *buffers, sems = refs
    copies = []
    for j, (views, start, size) in enumerate(jobs):
        flat_buf, value_buf = buffers[2 * j], buffers[2 * j + 1]
        rows = flat_buf.shape[1] // 2
        low_part, high_part = pl.ds(0, rows), pl.ds(rows, rows)
        targets = [
            flat_buf.at[:, low_part], flat_buf.at[:, high_part],
            value_buf.at[0, low_part], value_buf.at[0, high_part],
            value_buf.at[1, low_part], value_buf.at[1, high_part],
        ]
        copies.append([
            pltpu.make_async_copy(view(source, place_ref), target, sems.at[6 * j + i])
            for i, (view, source, target) in enumerate(zip(views, sources[6 * j : 6 * j + 6], targets))
        ])
    for group in copies:
        for copy in group:
            copy.start()
    for j, (_, start, size) in enumerate(jobs):
        flat_buf, value_buf = buffers[2 * j], buffers[2 * j + 1]
        for t in range(2):
            for copy in copies[j][2 + 2 * t : 4 + 2 * t] + (copies[j][:2] if t == 0 else []):
                copy.wait()
            value = dot_nn(flat_buf[...], value_buf[t])
            if stats_ref.shape[0] == value.shape[0]:
                edge = size - LANES
                store_rows(place_ref, t, outs, value[:, :edge], slice(start, start + edge))
                value = jnp.where(place_ref[0] == 0, value[:, edge:], stats_ref[...] + stats_got_ref[...])
                store_rows(place_ref, t, outs, value, slice(start + edge, start + size))
            else:
                store_rows(place_ref, t, outs, value, slice(start, start + size))


def weigh_call(place, stats, stats_got, *jobs):
    width, rows = jobs[0][0][0].shape
    cols = sum(job[2] for job in jobs)
    shape = (2, ZS, width // (2 * ZS), cols)
    bf = jnp.bfloat16
    arrays, plan, scratch, start = [], [], [], 0
    for values, views, size in jobs:
        arrays += values
        plan.append((views, start, size))
        scratch += [pltpu.VMEM((width, 2 * rows), bf), pltpu.VMEM((2, 2 * rows, size), bf)]
        start += size
    return pl.pallas_call(
        functools.partial(weigh_kernel, plan),
        in_specs=[pl.BlockSpec(memory_space=pltpu.SMEM)] + [pl.BlockSpec(memory_space=pltpu.VMEM)] * 2
        + [pl.BlockSpec(memory_space=pl.ANY)] * len(arrays),
        out_specs=[pl.BlockSpec(memory_space=pltpu.VMEM)] * 2,
        out_shape=[jax.ShapeDtypeStruct(shape, bf)] * 2,
        scratch_shapes=scratch + [pltpu.SemaphoreType.DMA((len(arrays),))],
        compiler_params=params(),
        cost_estimate=SMALL,
        name="weigh",
    )(place, stats, stats_got, *arrays)


def whole(ref, place_ref):
    return ref


def half_of(t, size):
    return lambda ref, place_ref: ref.at[:, pl.ds(t * size, size)]


def halved(flat, value, flat_got, value_got):
    size = value.shape[1] // 2
    views = [whole, whole, half_of(0, size), half_of(0, size), half_of(1, size), half_of(1, size)]
    return [flat, flat_got, value, value_got, value, value_got], views, size


def weigh(place, *args):
    none = jnp.zeros((8, LANES), jnp.float32)
    return weigh_call(place, none, none, halved(*args))


def weigh_more(place, flat, value, flat_got, value_got, flat_two, u, v, flat_two_got, u_got, v_got):
    own = lambda ref, place_ref: ref.at[place_ref[0]]
    views = [whole, whole, own, whole, own, whole]
    none = jnp.zeros((8, LANES), jnp.float32)
    return weigh_call(
        place, none, none,
        ([flat_two, flat_two_got, u, u_got, v, v_got], views, EDGE),
        halved(flat, value, flat_got, value_got),
    )


def weigh_last(place, flat, u, v, flat_got, u_got, v_got, stats, stats_got):
    return weigh_call(place, stats, stats_got, ([flat, flat_got, u, u_got, v, v_got], [whole] * 6, u.shape[1]))


def input_kernel(side_ref, mine_ref, other_ref, res_ref, um_ref, uo_ref, vm_ref, vo_ref, out_ref, mine, other, sems):
    @pl.when(pl.program_id(0) == 0)
    def _():
        load_halves(side_ref, mine_ref, other_ref, mine, other, sems)
        wait_set(mine, other, sems)

    total = res_ref[...]
    for t, (near, away) in enumerate(((um_ref, uo_ref), (vm_ref, vo_ref))):
        total = total + dot_nt(near[...], mine[t]) + dot_nt(away[...], other[t])
    out_ref[...] = low(total)


def input_back(resid, parts, weights):
    rows, width = resid.shape
    by_row = lambda n: pl.BlockSpec((BLOCK, n), lambda r: (r, 0))
    return pl.pallas_call(
        input_kernel,
        grid=(rows // BLOCK,),
        in_specs=set_specs() + [by_row(width)] + [by_row(parts[0][0].shape[1])] * 4,
        out_specs=by_row(width),
        out_shape=jax.ShapeDtypeStruct((rows, width), jnp.bfloat16),
        scratch_shapes=set_scratch(weights),
        compiler_params=params(),
        cost_estimate=SMALL,
        name="input_back",
    )(*set_args(weights), resid, *parts[0], *parts[1])


def halves(value):
    return jnp.split(value, 2, axis=-1)


def shards(
    tokens,
    segment,
    weight_qkv,
    weight_out,
    weight_in,
    weight_down,
    gain_one,
    shift_one,
    gain_two,
    shift_two,
    cotangent,
):
    rows, width = tokens.shape
    own = weight_qkv.shape[1]
    wide = weight_out.shape[0]
    half_span = weight_in.shape[1]
    bf = jnp.bfloat16

    norms = jnp.stack([gain_one, shift_one, gain_two, shift_two], axis=1)
    norms = jnp.pad(norms, ((0, 0), (0, LANES - 4)))
    set_one = jnp.concatenate([jnp.transpose(weight_qkv, (1, 0, 2)).reshape(own, -1), norms], axis=1)
    one = Flow(gather_steps(*halves(set_one)))
    one.go(2)
    weight_out, weight_in, weight_down, tokens, segment = sync(
        one, weight_out, weight_in, weight_down, tokens, segment
    )
    one.go()
    out_flat, half = weight_out.T, half_span // 2
    out_flat = jnp.pad(out_flat, ((0, 0), (0, 2 * EDGE - wide)))
    two = Flow(gather_steps(*[
        jnp.concatenate([o, w], axis=1) for o, w in zip(halves(out_flat), halves(weight_in))
    ]))
    three = Flow(gather_steps(*halves(weight_down.T)))
    two.go(2)
    three.go(2)
    numbers = lax.dynamic_slice_in_dim(segment, lax.axis_index("tensor") * rows, rows)
    numbers = numbers.reshape(-1, 1, SEQ), jnp.broadcast_to(numbers[:, None], (rows, LANES)).reshape(-1, SEQ, LANES)
    tokens, numbers = sync(one, two, three, tokens, numbers)
    one.go()
    sync(one, two)
    one.go()
    two.go()
    two.value = hold(two.value, one)
    one.go()
    one.go()
    sync(one, two)
    one.go()
    two.go()
    sync(one, two, three)
    one.go()
    two.go()
    tokens = sync(one, tokens)
    weights_one = one.go()
    kept = [attend(tokens, weights_one, numbers, 0, 0), None]
    tokens, kept[0] = sync(two, three, tokens, kept[0])
    two.go()
    tokens = sync(two, tokens)
    two.go()
    three.go()
    kept[0] = attend(tokens, weights_one, numbers, 0, 1, kept[0])
    tokens, kept[0] = sync(tokens, kept[0])
    kept[1] = attend(tokens, weights_one, numbers, 1, 0)
    tokens, kept[1] = sync(two, three, tokens, kept[1])
    two.go()
    three.go()
    tokens, kept[1] = sync(two, three, tokens, kept[1])
    two.go()
    three.go()
    first_mine, first_other, first_side = weights_one
    norms = jnp.where(first_side[0] == 0, first_other, first_mine)[:, 0, :, :, first_mine.shape[4] - LANES :]
    norms = jnp.transpose(norms, (1, 0, 2, 3)).reshape(width, LANES)[:, :8].T.astype(jnp.float32)
    kept[1] = attend(tokens, weights_one, numbers, 1, 1, kept[1])
    tokens, kept[1], norms = sync(two, three, tokens, kept[1], norms)
    three.go()
    tokens = sync(three, tokens)
    three.go()
    weights_two = two.go()
    attended = [kept[t][3] for t in range(2)]
    attended_got = [exchange(lax.dynamic_index_in_dim(value, 1 - core_side(), 0, keepdims=False)) for value in attended]
    total, tokens_flat, low_flat, *wide_out = widen(tokens, attended, weights_two, norms)
    hidden, slope = wide_out[:2], wide_out[2:]
    total, tokens_flat, low_flat, hidden, attended_got = sync(
        three, total, tokens_flat, low_flat, hidden, attended_got
    )
    three.go(2)
    weights_three = three.go()
    weights_three, away, low_flat, tokens_flat = sync(weights_three, hidden[1], low_flat, tokens_flat)
    hidden_got, low_got, tokens_got = exchange(away), exchange(low_flat), exchange(tokens_flat)
    output, second_flat, inner_mine, inner_other, grad_resid_one, grad_branch, branch_flat, stats = middle(
        total, hidden, slope, weights_three, weights_two, norms, cotangent
    )
    second_flat, hidden_got, low_got, tokens_got, inner_other, branch_flat, stats = sync(
        second_flat, hidden_got, low_got, tokens_got, inner_other, branch_flat, stats
    )
    second_got = exchange(second_flat)
    second_got, inner_other, branch_flat, stats = sync(second_got, inner_other, branch_flat, stats)
    inner_got, branch_got, stats_got = exchange(inner_other), exchange(branch_flat), exchange(stats)
    three = Flow(scatter_steps(lambda own: weigh(
        place_of(own), second_flat, hidden[0 if own else 1], second_got, hidden_got
    )))
    inner_mine, inner_got, branch_got, stats_got = sync(three, inner_mine, inner_got, branch_got, stats_got)
    three.go()
    two = Flow(scatter_steps(lambda own: weigh_more(
        place_of(own), low_flat, inner_mine if own else inner_other, low_got, inner_got,
        branch_flat, *attended, branch_got, *attended_got,
    )))
    grad_branch = sync(two, grad_branch)
    two.go()
    parts = [attend_back(grad_branch, weights_two, kept[0], 0)]
    parts[0] = sync(three, parts[0])
    three.go()
    grad_branch, kept[1], parts[0] = sync(three, grad_branch, kept[1], parts[0])
    three.go()
    parts_got = [exchange(parts[0][1])]
    parts.append(attend_back(grad_branch, weights_two, kept[1], 1))
    parts, parts_got = sync(two, three, parts, parts_got)
    parts_got.append(exchange(parts[1][1]))
    two.go()
    three.go()
    parts, parts_got = sync(two, three, parts, parts_got)
    two.go()
    three.go()
    one = Flow(scatter_steps(lambda own: weigh_last(
        place_of(own), tokens_flat, *[value[0 if own else 1] for value in parts], tokens_got, *parts_got, stats, stats_got
    )))
    grad_resid_one = sync(one, two, three, grad_resid_one)
    one.go()
    two.go()
    two.go()
    three.go(2)
    input_grad = input_back(grad_resid_one, parts, weights_one)
    input_grad = sync(one, two, input_grad)
    one.go()
    one.go()
    two.go(2)
    sync(one, two)
    one.go()
    one.go()
    one.go(2)
    sum_one = jnp.concatenate(one.go(), axis=1)
    two_left, two_right = two.go()
    sum_three = jnp.concatenate(three.go(), axis=1)
    stats = sum_one[:, 3 * wide : 3 * wide + 4].T
    sum_out = jnp.concatenate([two_left[:, :EDGE], two_right[:, :EDGE]], axis=1)[:, :wide]
    return (
        output,
        input_grad,
        jnp.transpose(sum_one[:, : 3 * wide].reshape(own, 3, -1), (1, 0, 2)),
        sum_out.T,
        jnp.concatenate([two_left[:, EDGE:], two_right[:, EDGE:]], axis=1),
        sum_three.T,
        stats[0],
        stats[1],
        stats[2],
        stats[3],
    )


def solution(mesh):
    both = P(("dp", "tensor"), None)
    split = P("dp")
    qkv_spec = P(None, "dp", "tensor")
    row_spec = P("tensor", "dp")
    in_spec = P("dp", "tensor")
    return jax.shard_map(
        shards,
        mesh=mesh,
        in_specs=(both, split, qkv_spec, row_spec, in_spec, row_spec, split, split, split, split, both),
        out_specs=(both, both, qkv_spec, row_spec, in_spec, row_spec, split, split, split, split),
        check_vma=False,
    )
```

profile of v0, /device:TPU:0, one launch (start us, length us, event | category | flops | bytes accessed | tf_op | source)
XLA Modules:
  0.0 305.1 jit_solution(14885809894745669340)
XLA Ops:
  0.7 1.0 copy.53
  3.0 0.9 collective-permute-done
  4.0 5.0 %collective-permute-start.1 = (bf16[96,640]{1,0:T(8,128)(2,1)S(1)}, bf16[96,640]{1,0:T(8,128)(2,1)S(1)}, u32[]{:S(2)}, u32[]{:S(2)}) collective-permute-start(bf16[96,640]{1,0:T(8,128)(2,1)S(1)} %maximum_select_fusion.9), channel_id=1, source_target_pairs={{0,24},{1,25},{2,26},{3,27},{4,28},{5,29},{6,30},{7,31},{8,0},{9,1... | collective-permute-start | bytes 368648 | tf_op jit(solution)/shard_map/ppermute | solution.py:56
  9.0 1.0 collective-permute-start.3
  10.0 0.9 fusion.14
  12.7 7.4 %collective-permute-done.2 = bf16[96,640]{1,0:T(8,128)(2,1)S(1)} collective-permute-done((bf16[96,640]{1,0:T(8,128)(2,1)S(1)}, bf16[96,640]{1,0:T(8,128)(2,1)S(1)}, u32[]{:S(2)}, u32[]{:S(2)}) %collective-permute-start.2) | collective-permute-done | bytes 122912 | tf_op jit(solution)/shard_map/ppermute | solution.py:56
  20.1 1.0 broadcast_in_dim.9.col_ref
  21.3 1.6 collective-permute-start.7
  23.3 7.5 %collective-permute-done.6 = bf16[96,1024]{1,0:T(8,128)(2,1)S(1)} collective-permute-done((bf16[96,1024]{1,0:T(8,128)(2,1)S(1)}, bf16[96,1024]{1,0:T(8,128)(2,1)S(1)}, u32[]{:S(2)}, u32[]{:S(2)}) %collective-permute-start.6) | collective-permute-done | bytes 196640 | tf_op jit(solution)/shard_map/ppermute | solution.py:56
  30.9 1.1 collective-permute-start.8
  32.1 2.2 collective-permute-start.10
  35.0 7.8 %collective-permute-done.10 = bf16[96,1024]{1,0:T(8,128)(2,1)S(1)} collective-permute-done((bf16[96,1024]{1,0:T(8,128)(2,1)S(1)}, bf16[96,1024]{1,0:T(8,128)(2,1)S(1)}, u32[]{:S(2)}, u32[]{:S(2)}) %collective-permute-start.10) | collective-permute-done | bytes 196640 | tf_op jit(solution)/shard_map/ppermute | solution.py:56
  43.2 2.0 collective-permute-done.8
  45.4 1.9 maximum_select_fusion.2.mine_ref
  47.4 1.6 collective-permute-start.11
  48.9 2.4 collective-permute-done.12.other_ref
  51.3 1.3 copy-done.2
  52.6 8.4 %attend.4 = (bf16[1,1024,640]{2,1,0:T(8,128)(2,1)}, bf16[1,1024,512]{2,1,0:T(8,128)(2,1)}, bf16[2,3,512,1024]{3,2,1,0:T(8,128)(2,1)}, bf16[2,1024,256]{2,1,0:T(8...) custom-call(s32[1]{0:T(128)} %bitcast.22.side_ref.side_two_ref, ...), custom_call_target="tpu_custom_call" | custom-call | flops 100000000 | bytes 100000 | tf_op jit(solution)/shard_map/attend/pallas_call | solution.py:322
  61.3 1.1 collective-permute-start.13
  62.4 2.6 collective-permute-start.14
  65.8 1.1 collective-permute-start.16
  67.0 8.5 %attend.5 = (bf16[1,1024,640]{2,1,0:T(8,128)(2,1)}, bf16[1,1024,512]{2,1,0:T(8,128)(2,1)}, bf16[2,3,512,1024]{3,2,1,0:T(8,128)(2,1)}, bf16[2,1024,256]{2,1,0:T(8...) custom-call(s32[1]{0:T(128)} %bitcast.22.side_ref.side_two_ref, ...), custom_call_target="tpu_custom_call", output_to_operand_aliasing={{0}: (6, {}), {1}: (7, {}), {2}: (8, {}), {3}: (9, {}), {4}... | custom-call | flops 100000000 | bytes 100000 | tf_op jit(solution)/shard_map/attend/pallas_call | solution.py:322
  75.5 8.3 %attend.6 = (bf16[1,1024,640]{2,1,0:T(8,128)(2,1)}, bf16[1,1024,512]{2,1,0:T(8,128)(2,1)}, bf16[2,3,512,1024]{3,2,1,0:T(8,128)(2,1)}, bf16[2,1024,256]{2,1,0:T(8...) custom-call(s32[1]{0:T(128)} %bitcast.22.side_ref.side_two_ref, ...), custom_call_target="tpu_custom_call" | custom-call | flops 100000000 | bytes 100000 | tf_op jit(solution)/shard_map/attend/pallas_call | solution.py:322
  84.1 0.9 constant_dynamic-slice_fusion
  84.9 1.0 maximum_select_fusion.mine_ref.mine_two_ref
  86.0 1.5 collective-permute-start.18
  87.6 1.1 fusion.9
  89.4 8.3 %attend.7 = (bf16[1,1024,640]{2,1,0:T(8,128)(2,1)}, bf16[1,1024,512]{2,1,0:T(8,128)(2,1)}, bf16[2,3,512,1024]{3,2,1,0:T(8,128)(2,1)}, bf16[2,1024,256]{2,1,0:T(8...) custom-call(s32[1]{0:T(128)} %bitcast.22.side_ref.side_two_ref, ...), custom_call_target="tpu_custom_call", output_to_operand_aliasing={{0}: (6, {}), {1}: (7, {}), {2}: (8, {}), {3}: (9, {}), {4}... | custom-call | flops 100000000 | bytes 100000 | tf_op jit(solution)/shard_map/attend/pallas_call | solution.py:322
  97.8 1.9 maximum_select_fusion.4
  100.3 1.1 dynamic-slice_bitcast_fusion.3
  102.0 19.7 %widen.1 = (f32[1024,768]{1,0:T(8,128)}, bf16[768,1024]{1,0:T(8,128)(2,1)}, bf16[768,1024]{1,0:T(8,128)(2,1)}, bf16[1024,1536]{1,0:T(8,128)(2,1)}, bf16[1024,153...) custom-call(s32[1]{0:T(128)} %bitcast.22.side_ref.side_two_ref, ...), custom_call_target="tpu_custom_call" | custom-call | flops 100000000 | bytes 100000 | tf_op jit(solution)/shard_map/widen/pallas_call | solution.py:500
  121.8 0.8 copy-done.17
  123.0 2.0 maximum_select_fusion.1.mine_ref
  125.1 4.5 %collective-permute-done.22.other_ref = bf16[2,2,4,96,768]{4,3,2,1,0:T(8,128)(2,1)S(1)} collective-permute-done((bf16[2,2,4,96,768]{4,3,2,1,0:T(8,128)(2,1)S(1)}, bf16[2,2,4,96,768]{4,3,2,1,0:T(8,128)(2,1)S(1)}, u32[]{:S(2)}, u32[]{:S(2)}) %collective-permute-start.22) | collective-permute-done | bytes 2359328 | tf_op jit(solution)/shard_map/ppermute | solution.py:56
  131.0 33.2 %middle.1 = (bf16[1024,768]{1,0:T(8,128)(2,1)}, bf16[768,1024]{1,0:T(8,128)(2,1)}, bf16[1024,1536]{1,0:T(8,128)(2,1)}, bf16[1024,1536]{1,0:T(8,128)(2,1)}, f32[1...) custom-call(s32[1]{0:T(128)} %bitcast.22.side_ref.side_two_ref, ...), custom_call_target="tpu_custom_call" | custom-call | flops 100000000 | bytes 100000 | tf_op jit(solution)/shard_map/middle/pallas_call | solution.py:578
  164.5 3.5 %collective-permute-done.26.refs_1_ = bf16[768,1024]{1,0:T(8,128)(2,1)S(1)} collective-permute-done((bf16[768,1024]{1,0:T(8,128)(2,1)}, bf16[768,1024]{1,0:T(8,128)(2,1)S(1)}, u32[]{:S(2)}, u32[]{:S(2)}) %collective-permute-start.26) | collective-permute-done | bytes 1572896 | tf_op jit(solution)/shard_map/ppermute | solution.py:56
  168.0 1.2 copy-done.9
  171.0 12.2 %weigh.3 = (bf16[2,4,96,768]{3,2,1,0:T(8,128)(2,1)}, bf16[2,4,96,768]{3,2,1,0:T(8,128)(2,1)}) custom-call(s32[2]{0:T(128)} %pad_add_fusion.place_ref, f32[8,128]{1,0:T(8,128)} %broadcast_1_stats_ref_stats_got_ref.2.stats_ref.stats_got_ref, f32[8,128]{1,0:T(8,128)} %broadcast_1_stats_ref_stats_got_ref.2.stats_ref.stats_got_ref, ...), custom_call_target="tpu_custom_call" | custom-call | flops 100000000 | bytes 100000 | tf_op jit(solution)/shard_map/weigh/pallas_call | solution.py:670
  183.3 1.2 copy-done.8
  184.5 1.5 collective-permute-start.31
  186.1 15.9 %weigh.4 = (bf16[2,4,96,1024]{3,2,1,0:T(8,128)(2,1)}, bf16[2,4,96,1024]{3,2,1,0:T(8,128)(2,1)}) custom-call(s32[2]{0:T(128)} %pad_add_fusion.place_ref, f32[8,128]{1,0:T(8,128)} %broadcast_1_stats_ref_stats_got_ref.2.stats_ref.stats_got_ref, f32[8,128]{1,0:T(8,128)} %broadcast_1_stats_ref_stats_got_ref.2.stats_ref.stats_got_ref, ...), custom_call_target="tpu_custom_call" | custom-call | flops 100000000 | bytes 100000 | tf_op jit(solution)/shard_map/weigh/pallas_call | solution.py:670
  202.1 1.6 collective-permute-start.30
  203.7 13.0 %attend_back.2 = (bf16[1024,640]{1,0:T(8,128)(2,1)}, bf16[1024,640]{1,0:T(8,128)(2,1)}) custom-call(s32[1]{0:T(128)} %bitcast.22.side_ref.side_two_ref, bf16[2,2,4,96,1024]{4,3,2,1,0:T(8,128)(2,1)} %copy-done, bf16[2,2,4,96,1024]{4,3,2,1,0:T(8,128)(2,1)} %collective-permute-done.17.other_ref.other_two_ref, bf16[1024,768]{1,0:T(8,128)(2,1)} %get-tuple-element.369.g_ref, ...), custom_call_target="tpu_custom_call" | custom-call | flops 100000000 | bytes 100000 | tf_op jit(solution)/shard_map/attend_back/pallas_call | solution.py:423
  216.7 1.7 add_convert_fusion.1
  218.5 1.0 collective-permute-start.32
  219.5 12.9 %attend_back.3 = (bf16[1024,640]{1,0:T(8,128)(2,1)}, bf16[1024,640]{1,0:T(8,128)(2,1)}) custom-call(s32[1]{0:T(128)} %bitcast.22.side_ref.side_two_ref, bf16[2,2,4,96,1024]{4,3,2,1,0:T(8,128)(2,1)} %copy-done, bf16[2,2,4,96,1024]{4,3,2,1,0:T(8,128)(2,1)} %collective-permute-done.17.other_ref.other_two_ref, bf16[1024,768]{1,0:T(8,128)(2,1)} %get-tuple-element.369.g_ref, ...), custom_call_target="tpu_custom_call" | custom-call | flops 100000000 | bytes 100000 | tf_op jit(solution)/shard_map/attend_back/pallas_call | solution.py:423
  232.4 0.8 copy-done.15
  233.2 1.6 fusion.1
  235.6 2.6 add_convert_fusion
  238.2 1.0 dynamic-slice_bitcast_fusion
  239.2 1.1 collective-permute-start.35
  240.3 2.4 collective-permute-start.36
  243.3 12.9 %weigh.5 = (bf16[2,4,96,640]{3,2,1,0:T(8,128)(2,1)}, bf16[2,4,96,640]{3,2,1,0:T(8,128)(2,1)}) custom-call(s32[2]{0:T(128)} %pad_add_fusion.place_ref, f32[768,128]{1,0:T(8,128)} %get-tuple-element.329.stats_ref, f32[768,128]{1,0:T(8,128)} %copy-done.18, bf16[768,1024]{1,0:T(8,128)(2,1)} %get-tuple-element.321.refs_0_, ...), custom_call_target="tpu_custom_call" | custom-call | flops 100000000 | bytes 100000 | tf_op jit(solution)/shard_map/weigh/pallas_call | solution.py:670
  256.4 1.1 collective-permute-start.39
  258.0 3.6 %collective-permute-start.40 = (bf16[96,1024]{1,0:T(8,128)(2,1)S(1)}, bf16[96,1024]{1,0:T(8,128)(2,1)S(1)}, u32[]{:S(2)}, u32[]{:S(2)}) collective-permute-start(bf16[96,1024]{1,0:T(8,128)(2,1)S(1)} %get-tuple-element.438), channel_id=1, source_target_pairs={{0,24},{1,25},{2,26},{3,27},{4,28},{5,29},{6,30},{7,31},{8,0},{9,1... | collective-permute-start | bytes 589832 | tf_op jit(solution)/shard_map/ppermute | solution.py:56
  261.6 0.8 collective-permute-start.41
  262.4 10.5 %input_back.1 = bf16[1024,768]{1,0:T(8,128)(2,1)} custom-call(s32[1]{0:T(128)} %bitcast.22.side_ref.side_two_ref, bf16[2,2,4,96,640]{4,3,2,1,0:T(8,128)(2,1)} %copy-done.1, bf16[2,2,4,96,640]{4,3,2,1,0:T(8,128)(2,1)} %copy-done.2, f32[1024,768]{1,0:T(8,128)} %get-tuple-element.396.res_ref, bf16[1024,640]{1,0:T(8,128)(2,1)} %get-tuple-element.384.refs_2_.um_ref, ...), custom_call_target="tpu_custom_call" | custom-call | flops 100000000 | bytes 100000 | tf_op jit(solution)/shard_map/input_back/pallas_call | solution.py:732
  273.0 7.4 %collective-permute-done.41 = bf16[96,1024]{1,0:T(8,128)(2,1)S(1)} collective-permute-done((bf16[96,1024]{1,0:T(8,128)(2,1)S(1)}, bf16[96,1024]{1,0:T(8,128)(2,1)S(1)}, u32[]{:S(2)}, u32[]{:S(2)}) %collective-permute-start.41) | collective-permute-done | bytes 196640 | tf_op jit(solution)/shard_map/ppermute | solution.py:56
  280.7 1.0 collective-permute-start.43
  283.3 6.2 %collective-permute-done.43 = bf16[4,96,640]{2,1,0:T(8,128)(2,1)S(1)} collective-permute-done((bf16[4,96,640]{2,1,0:T(8,128)(2,1)S(1)}, bf16[4,96,640]{2,1,0:T(8,128)(2,1)S(1)}, u32[]{:S(2)}, u32[]{:S(2)}) %collective-permute-start.43) | collective-permute-done | bytes 491552 | tf_op jit(solution)/shard_map/ppermute | solution.py:56
  289.8 1.4 collective-permute-start.46
  291.2 1.9 collective-permute-start.47
  293.2 1.6 collective-permute-done.45
  294.9 6.6 %collective-permute-done.46 = bf16[96,640]{1,0:T(8,128)(2,1)S(1)} collective-permute-done((bf16[96,640]{1,0:T(8,128)(2,1)S(1)}, bf16[96,640]{1,0:T(8,128)(2,1)S(1)}, u32[]{:S(2)}, u32[]{:S(2)}) %collective-permute-start.46) | collective-permute-done | bytes 122912 | tf_op jit(solution)/shard_map/ppermute | solution.py:56
  (180 shorter events, 20.1 us)
Async XLA Ops:
  0.6 11.0 %copy-start.22 = (s32[2048]{0:T(1024)S(1)}, s32[2048]{0:T(1024)}, u32[]{:S(2)}) copy-start(s32[2048]{0:T(1024)} %param.12) | copy-start | bytes 24580
  0.7 10.4 %copy-start.21 = (bf16[384,48]{0,1:T(8,128)(2,1)S(1)}, bf16[384,48]{0,1:T(8,128)(2,1)}, u32[]{:S(2)}) copy-start(bf16[384,48]{0,1:T(8,128)(2,1)} %param.14) | copy-start | bytes 110596
  0.7 10.4 %copy-start.19 = (bf16[48,1536]{1,0:T(8,128)(2,1)S(1)}, bf16[48,1536]{1,0:T(8,128)(2,1)}, u32[]{:S(2)}) copy-start(bf16[48,1536]{1,0:T(8,128)(2,1)} %param.15) | copy-start | bytes 442372
  2.5 1.4 collective-permute-start
  4.0 8.7 %collective-permute-start.1 = (bf16[96,640]{1,0:T(8,128)(2,1)S(1)}, bf16[96,640]{1,0:T(8,128)(2,1)S(1)}, u32[]{:S(2)}, u32[]{:S(2)}) collective-permute-start(bf16[96,640]{1,0:T(8,128)(2,1)S(1)} %maximum_select_fusion.9), channel_id=1, source_target_pairs={{0,24},{1,25},{2,26},{3,27},{4,28},{5,29},{6,30},{7,31},{8,0},{9,1... | collective-permute-start | bytes 368648 | tf_op jit(solution)/shard_map/ppermute | solution.py:56
  9.0 11.1 %collective-permute-start.2 = (bf16[96,640]{1,0:T(8,128)(2,1)S(1)}, bf16[96,640]{1,0:T(8,128)(2,1)S(1)}, u32[]{:S(2)}, u32[]{:S(2)}) collective-permute-start(bf16[96,640]{1,0:T(8,128)(2,1)S(1)} %maximum_select_fusion.9), channel_id=1, source_target_pairs={{0,16},{1,17},{2,18},{3,19},{4,20},{5,21},{6,22},{7,23},{8,24},{9,... | collective-permute-start | bytes 368648 | tf_op jit(solution)/shard_map/ppermute | solution.py:56
  9.0 11.1 %collective-permute-start.3 = (bf16[96,640]{1,0:T(8,128)(2,1)S(1)}, bf16[96,640]{1,0:T(8,128)(2,1)S(1)}, u32[]{:S(2)}, u32[]{:S(2)}) collective-permute-start(bf16[96,640]{1,0:T(8,128)(2,1)S(1)} %maximum_select_fusion.9), channel_id=1, source_target_pairs={{0,8},{1,9},{2,10},{3,11},{4,12},{5,13},{6,14},{7,15},{8,16},{9,17... | collective-permute-start | bytes 368648 | tf_op jit(solution)/shard_map/ppermute | solution.py:56
  10.9 1.3 collective-permute-start.5
  11.1 1.5 collective-permute-start.4
  11.7 9.6 %copy-start.20 = (s32[1024]{0:T(1024)}, s32[1024]{0:T(1024)S(1)}, u32[]{:S(2)}) copy-start(s32[1024]{0:T(1024)S(1)} %dynamic_slice.100) | copy-start | bytes 12292
  21.3 9.5 %collective-permute-start.7 = (bf16[4,96,640]{2,1,0:T(8,128)(2,1)S(1)}, bf16[4,96,640]{2,1,0:T(8,128)(2,1)S(1)}, u32[]{:S(2)}, u32[]{:S(2)}) collective-permute-start(bf16[4,96,640]{2,1,0:T(8,128)(2,1)S(1)} %constant_dynamic-slice_fusion.2), channel_id=1, source_target_pairs={{0,4},{1,5},{2,3},{3,2},{4,0},{5,1},{6,7},{7,6},{8,12},{9,13},{10,... | collective-permute-start | bytes 1474568 | tf_op jit(solution)/shard_map/ppermute | solution.py:56
  22.8 7.9 %collective-permute-start.6 = (bf16[96,1024]{1,0:T(8,128)(2,1)S(1)}, bf16[96,1024]{1,0:T(8,128)(2,1)S(1)}, u32[]{:S(2)}, u32[]{:S(2)}) collective-permute-start(bf16[96,1024]{1,0:T(8,128)(2,1)S(1)} %maximum_select_fusion.7), channel_id=1, source_target_pairs={{0,8},{1,9},{2,10},{3,11},{4,12},{5,13},{6,14},{7,15},{8,16},{9,17... | collective-permute-start | bytes 589832 | tf_op jit(solution)/shard_map/ppermute | solution.py:56
  30.9 14.3 %collective-permute-start.8 = (bf16[2,4,96,640]{3,2,1,0:T(8,128)(2,1)S(1)}, bf16[2,4,96,640]{3,2,1,0:T(8,128)(2,1)}, u32[]{:S(2)}, u32[]{:S(2)}) collective-permute-start(bf16[2,4,96,640]{3,2,1,0:T(8,128)(2,1)S(1)} %maximum_select_fusion.6), channel_id=1, source_target_pairs={{0,1},{1,0},{2,6},{3,7},{4,5},{5,4},{6,2},{7,3},{8,9},{9,8},{10,14... | collective-permute-start | bytes 2949128 | tf_op jit(solution)/shard_map/ppermute | solution.py:56
  32.1 10.7 %collective-permute-start.10 = (bf16[96,1024]{1,0:T(8,128)(2,1)S(1)}, bf16[96,1024]{1,0:T(8,128)(2,1)S(1)}, u32[]{:S(2)}, u32[]{:S(2)}) collective-permute-start(bf16[96,1024]{1,0:T(8,128)(2,1)S(1)} %maximum_select_fusion.7), channel_id=1, source_target_pairs={{0,16},{1,17},{2,18},{3,19},{4,20},{5,21},{6,22},{7,23},{8,24},{9,... | collective-permute-start | bytes 589832 | tf_op jit(solution)/shard_map/ppermute | solution.py:56
  34.3 8.9 %collective-permute-start.9 = (bf16[96,1024]{1,0:T(8,128)(2,1)S(1)}, bf16[96,1024]{1,0:T(8,128)(2,1)S(1)}, u32[]{:S(2)}, u32[]{:S(2)}) collective-permute-start(bf16[96,1024]{1,0:T(8,128)(2,1)S(1)} %maximum_select_fusion.7), channel_id=1, source_target_pairs={{0,24},{1,25},{2,26},{3,27},{4,28},{5,29},{6,30},{7,31},{8,0},{9,1... | collective-permute-start | bytes 589832 | tf_op jit(solution)/shard_map/ppermute | solution.py:56
  47.3 4.1 %copy-start.1 = (bf16[2,2,4,96,640]{4,3,2,1,0:T(8,128)(2,1)}, bf16[2,2,4,96,640]{4,3,2,1,0:T(8,128)(2,1)S(1)}, u32[]{:S(2)}) copy-start(bf16[2,2,4,96,640]{4,3,2,1,0:T(8,128)(2,1)S(1)} %maximum_select_fusion.2.mine_ref) | copy-start | bytes 5898244
  47.3 4.0 %collective-permute-start.12 = (bf16[2,2,4,96,640]{4,3,2,1,0:T(8,128)(2,1)S(1)}, bf16[2,2,4,96,640]{4,3,2,1,0:T(8,128)(2,1)S(1)}, u32[]{:S(2)}, u32[]{:S(2)}) collective-permute-start(bf16[2,2,4,96,640]{4,3,2,1,0:T(8,128)(2,1)S(1)} %maximum_select_fusion.2.mine_ref), channel_id=1, source_target_pairs={{0,2},{1,3},{2,0},{3,1},{4,6},{5,7},{6,4},{7,5},{8,10},{9,11},{10,... | collective-permute-start | bytes 5898248 | tf_op jit(solution)/shard_map/ppermute | solution.py:56
  47.4 13.6 %collective-permute-start.11 = (bf16[4,96,1024]{2,1,0:T(8,128)(2,1)S(1)}, bf16[4,96,1024]{2,1,0:T(8,128)(2,1)S(1)}, u32[]{:S(2)}, u32[]{:S(2)}) collective-permute-start(bf16[4,96,1024]{2,1,0:T(8,128)(2,1)S(1)} %constant_dynamic-slice_fusion.1), channel_id=1, source_target_pairs={{0,4},{1,5},{2,3},{3,2},{4,0},{5,1},{6,7},{7,6},{8,12},{9,13},{10,... | collective-permute-start | bytes 2359304 | tf_op jit(solution)/shard_map/ppermute | solution.py:56
  61.3 22.6 %collective-permute-start.13 = (bf16[2,4,96,1024]{3,2,1,0:T(8,128)(2,1)S(1)}, bf16[2,4,96,1024]{3,2,1,0:T(8,128)(2,1)S(1)}, u32[]{:S(2)}, u32[]{:S(2)}) collective-permute-start(bf16[2,4,96,1024]{3,2,1,0:T(8,128)(2,1)S(1)} %maximum_select_fusion.3), channel_id=1, source_target_pairs={{0,1},{1,0},{2,6},{3,7},{4,5},{5,4},{6,2},{7,3},{8,9},{9,8},{10,14... | collective-permute-start | bytes 4718600 | tf_op jit(solution)/shard_map/ppermute | solution.py:56
  62.4 21.5 %collective-permute-start.14 = (bf16[96,768]{1,0:T(8,128)(2,1)S(1)}, bf16[96,768]{1,0:T(8,128)(2,1)S(1)}, u32[]{:S(2)}, u32[]{:S(2)}) collective-permute-start(bf16[96,768]{1,0:T(8,128)(2,1)S(1)} %maximum_select_fusion.8), channel_id=1, source_target_pairs={{0,24},{1,25},{2,26},{3,27},{4,28},{5,29},{6,30},{7,31},{8,0},{9,1... | collective-permute-start | bytes 442376 | tf_op jit(solution)/shard_map/ppermute | solution.py:56
  65.0 18.9 %collective-permute-start.15 = (bf16[96,768]{1,0:T(8,128)(2,1)S(1)}, bf16[96,768]{1,0:T(8,128)(2,1)S(1)}, u32[]{:S(2)}, u32[]{:S(2)}) collective-permute-start(bf16[96,768]{1,0:T(8,128)(2,1)S(1)} %maximum_select_fusion.8), channel_id=1, source_target_pairs={{0,16},{1,17},{2,18},{3,19},{4,20},{5,21},{6,22},{7,23},{8,24},{9,... | collective-permute-start | bytes 442376 | tf_op jit(solution)/shard_map/ppermute | solution.py:56
  65.8 18.1 %collective-permute-start.16 = (bf16[96,768]{1,0:T(8,128)(2,1)S(1)}, bf16[96,768]{1,0:T(8,128)(2,1)S(1)}, u32[]{:S(2)}, u32[]{:S(2)}) collective-permute-start(bf16[96,768]{1,0:T(8,128)(2,1)S(1)} %maximum_select_fusion.8), channel_id=1, source_target_pairs={{0,8},{1,9},{2,10},{3,11},{4,12},{5,13},{6,14},{7,15},{8,16},{9,17... | collective-permute-start | bytes 442376 | tf_op jit(solution)/shard_map/ppermute | solution.py:56
  86.0 11.8 %copy-start = (bf16[2,2,4,96,1024]{4,3,2,1,0:T(8,128)(2,1)}, bf16[2,2,4,96,1024]{4,3,2,1,0:T(8,128)(2,1)S(1)}, u32[]{:S(2)}) copy-start(bf16[2,2,4,96,1024]{4,3,2,1,0:T(8,128)(2,1)S(1)} %maximum_select_fusion.mine_ref.mine_two_ref) | copy-start | bytes 9437188
  86.0 11.8 %collective-permute-start.17 = (bf16[2,2,4,96,1024]{4,3,2,1,0:T(8,128)(2,1)S(1)}, bf16[2,2,4,96,1024]{4,3,2,1,0:T(8,128)(2,1)}, u32[]{:S(2)}, u32[]{:S(2)}) collective-permute-start(bf16[2,2,4,96,1024]{4,3,2,1,0:T(8,128)(2,1)S(1)} %maximum_select_fusion.mine_ref.mine_two_ref), channel_id=1, source_target_pairs={{0,2},{1,3},{2,0},{3,1},{4,6},{5,7},{6,4},{7,5},{8,10},{9,11},{10,... | collective-permute-start | bytes 9437192 | tf_op jit(solution)/shard_map/ppermute | solution.py:56
  86.0 11.7 %collective-permute-start.18 = (bf16[4,96,768]{2,1,0:T(8,128)(2,1)}, bf16[4,96,768]{2,1,0:T(8,128)(2,1)}, u32[]{:S(2)}, u32[]{:S(2)}) collective-permute-start(bf16[4,96,768]{2,1,0:T(8,128)(2,1)} %constant_dynamic-slice_fusion), channel_id=1, source_target_pairs={{0,4},{1,5},{2,3},{3,2},{4,0},{5,1},{6,7},{7,6},{8,12},{9,13},{10,... | collective-permute-start | bytes 1769480 | tf_op jit(solution)/shard_map/ppermute | solution.py:56
  97.8 3.6 %copy-start.3 = (bf16[2,1024,256]{2,1,0:T(8,128)(2,1)S(1)}, bf16[2,1024,256]{2,1,0:T(8,128)(2,1)}, u32[]{:S(2)}) copy-start(bf16[2,1024,256]{2,1,0:T(8,128)(2,1)} %get-tuple-element.299.v_ref.refs_4_) | copy-start | bytes 3145732
  99.7 22.1 %collective-permute-start.19 = (bf16[2,4,96,768]{3,2,1,0:T(8,128)(2,1)S(1)}, bf16[2,4,96,768]{3,2,1,0:T(8,128)(2,1)S(1)}, u32[]{:S(2)}, u32[]{:S(2)}) collective-permute-start(bf16[2,4,96,768]{3,2,1,0:T(8,128)(2,1)S(1)} %maximum_select_fusion.4), channel_id=1, source_target_pairs={{0,1},{1,0},{2,6},{3,7},{4,5},{5,4},{6,2},{7,3},{8,9},{9,8},{10,14... | collective-permute-start | bytes 3538952 | tf_op jit(solution)/shard_map/ppermute | solution.py:56
  101.4 20.4 %collective-permute-start.20 = (bf16[1024,256]{1,0:T(8,128)(2,1)S(1)}, bf16[1024,256]{1,0:T(8,128)(2,1)S(1)}, u32[]{:S(2)}, u32[]{:S(2)}) collective-permute-start(bf16[1024,256]{1,0:T(8,128)(2,1)S(1)} %dynamic-slice_bitcast_fusion.3), channel_id=1, source_target_pairs={{0,2},{1,3},{2,0},{3,1},{4,6},{5,7},{6,4},{7,5},{8,10},{9,11},{10,... | collective-permute-start | bytes 1572872 | tf_op jit(solution)/shard_map/ppermute | solution.py:56
  101.5 20.3 %collective-permute-start.21 = (bf16[1024,256]{1,0:T(8,128)(2,1)S(1)}, bf16[1024,256]{1,0:T(8,128)(2,1)S(1)}, u32[]{:S(2)}, u32[]{:S(2)}) collective-permute-start(bf16[1024,256]{1,0:T(8,128)(2,1)S(1)} %dynamic-slice_bitcast_fusion.2), channel_id=1, source_target_pairs={{0,2},{1,3},{2,0},{3,1},{4,6},{5,7},{6,4},{7,5},{8,10},{9,11},{10,... | collective-permute-start | bytes 1572872 | tf_op jit(solution)/shard_map/ppermute | solution.py:56
  121.8 3.3 %copy-start.16 = (bf16[1024,256]{1,0:T(8,128)(2,1)}, bf16[1024,256]{1,0:T(8,128)(2,1)S(1)}, u32[]{:S(2)}) copy-start(bf16[1024,256]{1,0:T(8,128)(2,1)S(1)} %collective-permute-done.20.refs_3_) | copy-start | bytes 1572868
  125.0 5.3 %copy-start.6 = (bf16[2,2,4,96,768]{4,3,2,1,0:T(8,128)(2,1)}, bf16[2,2,4,96,768]{4,3,2,1,0:T(8,128)(2,1)S(1)}, u32[]{:S(2)}) copy-start(bf16[2,2,4,96,768]{4,3,2,1,0:T(8,128)(2,1)S(1)} %maximum_select_fusion.1.mine_ref) | copy-start | bytes 7077892
  125.0 4.6 %collective-permute-start.22 = (bf16[2,2,4,96,768]{4,3,2,1,0:T(8,128)(2,1)S(1)}, bf16[2,2,4,96,768]{4,3,2,1,0:T(8,128)(2,1)S(1)}, u32[]{:S(2)}, u32[]{:S(2)}) collective-permute-start(bf16[2,2,4,96,768]{4,3,2,1,0:T(8,128)(2,1)S(1)} %maximum_select_fusion.1.mine_ref), channel_id=1, source_target_pairs={{0,2},{1,3},{2,0},{3,1},{4,6},{5,7},{6,4},{7,5},{8,10},{9,11},{10,... | collective-permute-start | bytes 7077896 | tf_op jit(solution)/shard_map/ppermute | solution.py:56
  129.6 34.7 %collective-permute-start.23 = (bf16[1024,1536]{1,0:T(8,128)(2,1)}, bf16[1024,1536]{1,0:T(8,128)(2,1)S(1)}, u32[]{:S(2)}, u32[]{:S(2)}) collective-permute-start(bf16[1024,1536]{1,0:T(8,128)(2,1)} %get-tuple-element.319.ho_ref), channel_id=1, source_target_pairs={{0,2},{1,3},{2,0},{3,1},{4,6},{5,7},{6,4},{7,5},{8,10},{9,11},{10,... | collective-permute-start | bytes 9437192 | tf_op jit(solution)/shard_map/ppermute | solution.py:56
  129.7 34.5 %collective-permute-start.24 = (bf16[768,1024]{1,0:T(8,128)(2,1)}, bf16[768,1024]{1,0:T(8,128)(2,1)}, u32[]{:S(2)}, u32[]{:S(2)}) collective-permute-start(bf16[768,1024]{1,0:T(8,128)(2,1)} %get-tuple-element.320.refs_6_), channel_id=1, source_target_pairs={{0,2},{1,3},{2,0},{3,1},{4,6},{5,7},{6,4},{7,5},{8,10},{9,11},{10,... | collective-permute-start | bytes 4718600 | tf_op jit(solution)/shard_map/ppermute | solution.py:56
  130.1 34.2 %collective-permute-start.25 = (bf16[768,1024]{1,0:T(8,128)(2,1)}, bf16[768,1024]{1,0:T(8,128)(2,1)}, u32[]{:S(2)}, u32[]{:S(2)}) collective-permute-start(bf16[768,1024]{1,0:T(8,128)(2,1)} %get-tuple-element.321.refs_0_), channel_id=1, source_target_pairs={{0,2},{1,3},{2,0},{3,1},{4,6},{5,7},{6,4},{7,5},{8,10},{9,11},{10,... | collective-permute-start | bytes 4718600 | tf_op jit(solution)/shard_map/ppermute | solution.py:56
  164.3 6.7 %copy-start.4 = (bf16[1024,1536]{1,0:T(8,128)(2,1)}, bf16[1024,1536]{1,0:T(8,128)(2,1)S(1)}, u32[]{:S(2)}) copy-start(bf16[1024,1536]{1,0:T(8,128)(2,1)S(1)} %collective-permute-done.23.refs_3_.refs_5_) | copy-start | bytes 9437188
  164.3 3.7 %collective-permute-start.26 = (bf16[768,1024]{1,0:T(8,128)(2,1)}, bf16[768,1024]{1,0:T(8,128)(2,1)S(1)}, u32[]{:S(2)}, u32[]{:S(2)}) collective-permute-start(bf16[768,1024]{1,0:T(8,128)(2,1)} %get-tuple-element.325.refs_0_), channel_id=1, source_target_pairs={{0,2},{1,3},{2,0},{3,1},{4,6},{5,7},{6,4},{7,5},{8,10},{9,11},{10,... | collective-permute-start | bytes 4718600 | tf_op jit(solution)/shard_map/ppermute | solution.py:56
  169.2 14.1 %collective-permute-start.27 = (bf16[1024,1536]{1,0:T(8,128)(2,1)}, bf16[1024,1536]{1,0:T(8,128)(2,1)S(1)}, u32[]{:S(2)}, u32[]{:S(2)}) collective-permute-start(bf16[1024,1536]{1,0:T(8,128)(2,1)} %get-tuple-element.334), channel_id=1, source_target_pairs={{0,2},{1,3},{2,0},{3,1},{4,6},{5,7},{6,4},{7,5},{8,10},{9,11},{10,... | collective-permute-start | bytes 9437192 | tf_op jit(solution)/shard_map/ppermute | solution.py:56
  169.3 14.0 %collective-permute-start.28 = (bf16[768,1024]{1,0:T(8,128)(2,1)}, bf16[768,1024]{1,0:T(8,128)(2,1)S(1)}, u32[]{:S(2)}, u32[]{:S(2)}) collective-permute-start(bf16[768,1024]{1,0:T(8,128)(2,1)} %get-tuple-element.335.refs_0_), channel_id=1, source_target_pairs={{0,2},{1,3},{2,0},{3,1},{4,6},{5,7},{6,4},{7,5},{8,10},{9,11},{10,... | collective-permute-start | bytes 4718600 | tf_op jit(solution)/shard_map/ppermute | solution.py:56
  169.7 13.6 %collective-permute-start.29 = (f32[768,128]{1,0:T(8,128)}, f32[768,128]{1,0:T(8,128)S(1)}, u32[]{:S(2)}, u32[]{:S(2)}) collective-permute-start(f32[768,128]{1,0:T(8,128)} %get-tuple-element.329.stats_ref), channel_id=1, source_target_pairs={{0,2},{1,3},{2,0},{3,1},{4,6},{5,7},{6,4},{7,5},{8,10},{9,11},{10,... | collective-permute-start | bytes 1179656 | tf_op jit(solution)/shard_map/ppermute | solution.py:56
  183.3 18.8 %copy-start.18 = (f32[768,128]{1,0:T(8,128)}, f32[768,128]{1,0:T(8,128)S(1)}, u32[]{:S(2)}) copy-start(f32[768,128]{1,0:T(8,128)S(1)} %collective-permute-done.29.stats_got_ref) | copy-start | bytes 1179652
  184.5 32.1 %collective-permute-start.31 = (bf16[2,4,96,768]{3,2,1,0:T(8,128)(2,1)}, bf16[2,4,96,768]{3,2,1,0:T(8,128)(2,1)}, u32[]{:S(2)}, u32[]{:S(2)}) collective-permute-start(bf16[2,4,96,768]{3,2,1,0:T(8,128)(2,1)} %get-tuple-element.349), channel_id=1, source_target_pairs={{0,1},{1,0},{2,6},{3,7},{4,5},{5,4},{6,2},{7,3},{8,9},{9,8},{10,14... | collective-permute-start | bytes 3538952 | tf_op jit(solution)/shard_map/ppermute | solution.py:56
  202.1 14.6 %copy-start.12 = (bf16[2,4,96,768]{3,2,1,0:T(8,128)(2,1)S(1)}, bf16[2,4,96,768]{3,2,1,0:T(8,128)(2,1)}, u32[]{:S(2)}) copy-start(bf16[2,4,96,768]{3,2,1,0:T(8,128)(2,1)} %get-tuple-element.348) | copy-start | bytes 3538948
  202.1 30.3 %collective-permute-start.30 = (bf16[2,4,96,1024]{3,2,1,0:T(8,128)(2,1)}, bf16[2,4,96,1024]{3,2,1,0:T(8,128)(2,1)}, u32[]{:S(2)}, u32[]{:S(2)}) collective-permute-start(bf16[2,4,96,1024]{3,2,1,0:T(8,128)(2,1)} %get-tuple-element.347), channel_id=1, source_target_pairs={{0,1},{1,0},{2,6},{3,7},{4,5},{5,4},{6,2},{7,3},{8,9},{9,8},{10,14... | collective-permute-start | bytes 4718600 | tf_op jit(solution)/shard_map/ppermute | solution.py:56
  218.4 14.0 %collective-permute-start.33 = (bf16[1024,640]{1,0:T(8,128)(2,1)S(1)}, bf16[1024,640]{1,0:T(8,128)(2,1)S(1)}, u32[]{:S(2)}, u32[]{:S(2)}) collective-permute-start(bf16[1024,640]{1,0:T(8,128)(2,1)S(1)} %copy-done.11), channel_id=1, source_target_pairs={{0,2},{1,3},{2,0},{3,1},{4,6},{5,7},{6,4},{7,5},{8,10},{9,11},{10,... | collective-permute-start | bytes 3932168 | tf_op jit(solution)/shard_map/ppermute | solution.py:56
  218.5 13.9 %collective-permute-start.32 = (bf16[4,96,768]{2,1,0:T(8,128)(2,1)S(1)}, bf16[4,96,768]{2,1,0:T(8,128)(2,1)S(1)}, u32[]{:S(2)}, u32[]{:S(2)}) collective-permute-start(bf16[4,96,768]{2,1,0:T(8,128)(2,1)S(1)} %dynamic-slice_bitcast_fusion.1), channel_id=1, source_target_pairs={{0,4},{1,5},{2,3},{3,2},{4,0},{5,1},{6,7},{7,6},{8,12},{9,13},{10,... | collective-permute-start | bytes 1769480 | tf_op jit(solution)/shard_map/ppermute | solution.py:56
  233.2 5.0 %copy-start.10 = (bf16[1024,640]{1,0:T(8,128)(2,1)}, bf16[1024,640]{1,0:T(8,128)(2,1)S(1)}, u32[]{:S(2)}) copy-start(bf16[1024,640]{1,0:T(8,128)(2,1)S(1)} %collective-permute-done.33.refs_3_) | copy-start | bytes 3932164
  233.2 6.0 %collective-permute-start.34 = (bf16[1024,640]{1,0:T(8,128)(2,1)}, bf16[1024,640]{1,0:T(8,128)(2,1)}, u32[]{:S(2)}, u32[]{:S(2)}) collective-permute-start(bf16[1024,640]{1,0:T(8,128)(2,1)} %get-tuple-element.398.vo_ref), channel_id=1, source_target_pairs={{0,2},{1,3},{2,0},{3,1},{4,6},{5,7},{6,4},{7,5},{8,10},{9,11},{10,... | collective-permute-start | bytes 3932168 | tf_op jit(solution)/shard_map/ppermute | solution.py:56
  239.2 17.1 %collective-permute-start.35 = (bf16[4,96,1024]{2,1,0:T(8,128)(2,1)}, bf16[4,96,1024]{2,1,0:T(8,128)(2,1)S(1)}, u32[]{:S(2)}, u32[]{:S(2)}) collective-permute-start(bf16[4,96,1024]{2,1,0:T(8,128)(2,1)} %dynamic-slice_bitcast_fusion), channel_id=1, source_target_pairs={{0,4},{1,5},{2,3},{3,2},{4,0},{5,1},{6,7},{7,6},{8,12},{9,13},{10,... | collective-permute-start | bytes 2359304 | tf_op jit(solution)/shard_map/ppermute | solution.py:56
  240.3 15.9 %collective-permute-start.36 = (bf16[96,768]{1,0:T(8,128)(2,1)}, bf16[96,768]{1,0:T(8,128)(2,1)S(1)}, u32[]{:S(2)}, u32[]{:S(2)}) collective-permute-start(bf16[96,768]{1,0:T(8,128)(2,1)} %get-tuple-element.390), channel_id=1, source_target_pairs={{0,24},{1,25},{2,26},{3,27},{4,28},{5,29},{6,30},{7,31},{8,0},{9,1... | collective-permute-start | bytes 442376 | tf_op jit(solution)/shard_map/ppermute | solution.py:56
  242.7 13.6 %collective-permute-start.37 = (bf16[96,768]{1,0:T(8,128)(2,1)}, bf16[96,768]{1,0:T(8,128)(2,1)S(1)}, u32[]{:S(2)}, u32[]{:S(2)}) collective-permute-start(bf16[96,768]{1,0:T(8,128)(2,1)} %get-tuple-element.391), channel_id=1, source_target_pairs={{0,16},{1,17},{2,18},{3,19},{4,20},{5,21},{6,22},{7,23},{8,24},{9,... | collective-permute-start | bytes 442376 | tf_op jit(solution)/shard_map/ppermute | solution.py:56
  243.1 13.3 %collective-permute-start.38 = (bf16[96,768]{1,0:T(8,128)(2,1)}, bf16[96,768]{1,0:T(8,128)(2,1)S(1)}, u32[]{:S(2)}, u32[]{:S(2)}) collective-permute-start(bf16[96,768]{1,0:T(8,128)(2,1)} %get-tuple-element.392), channel_id=1, source_target_pairs={{0,8},{1,9},{2,10},{3,11},{4,12},{5,13},{6,14},{7,15},{8,16},{9,17... | collective-permute-start | bytes 442376 | tf_op jit(solution)/shard_map/ppermute | solution.py:56
  256.4 24.0 %collective-permute-start.39 = (bf16[2,4,96,640]{3,2,1,0:T(8,128)(2,1)}, bf16[2,4,96,640]{3,2,1,0:T(8,128)(2,1)S(1)}, u32[]{:S(2)}, u32[]{:S(2)}) collective-permute-start(bf16[2,4,96,640]{3,2,1,0:T(8,128)(2,1)} %get-tuple-element.394), channel_id=1, source_target_pairs={{0,1},{1,0},{2,6},{3,7},{4,5},{5,4},{6,2},{7,3},{8,9},{9,8},{10,14... | collective-permute-start | bytes 2949128 | tf_op jit(solution)/shard_map/ppermute | solution.py:56
  257.5 15.4 %collective-permute-start.49 = (f32[48,768]{1,0:T(8,128)S(1)}, f32[48,768]{1,0:T(8,128)S(1)}, u32[]{:S(2)}, u32[]{:S(2)}) collective-permute-start(f32[48,768]{1,0:T(8,128)S(1)} %dynamic-slice_bitcast_fusion.9), channel_id=1, source_target_pairs={{0,2},{1,3},{2,0},{3,1},{4,6},{5,7},{6,4},{7,5},{8,10},{9,11},{10,... | collective-permute-start | bytes 442376 | tf_op jit(solution)/shard_map/ppermute | solution.py:56
  258.0 15.0 %collective-permute-start.40 = (bf16[96,1024]{1,0:T(8,128)(2,1)S(1)}, bf16[96,1024]{1,0:T(8,128)(2,1)S(1)}, u32[]{:S(2)}, u32[]{:S(2)}) collective-permute-start(bf16[96,1024]{1,0:T(8,128)(2,1)S(1)} %get-tuple-element.438), channel_id=1, source_target_pairs={{0,24},{1,25},{2,26},{3,27},{4,28},{5,29},{6,30},{7,31},{8,0},{9,1... | collective-permute-start | bytes 589832 | tf_op jit(solution)/shard_map/ppermute | solution.py:56
  261.6 18.7 %collective-permute-start.41 = (bf16[96,1024]{1,0:T(8,128)(2,1)S(1)}, bf16[96,1024]{1,0:T(8,128)(2,1)S(1)}, u32[]{:S(2)}, u32[]{:S(2)}) collective-permute-start(bf16[96,1024]{1,0:T(8,128)(2,1)S(1)} %get-tuple-element.437), channel_id=1, source_target_pairs={{0,16},{1,17},{2,18},{3,19},{4,20},{5,21},{6,22},{7,23},{8,24},{9,... | collective-permute-start | bytes 589832 | tf_op jit(solution)/shard_map/ppermute | solution.py:56
  262.4 17.9 %copy-start.14 = (bf16[2,4,96,640]{3,2,1,0:T(8,128)(2,1)S(1)}, bf16[2,4,96,640]{3,2,1,0:T(8,128)(2,1)}, u32[]{:S(2)}) copy-start(bf16[2,4,96,640]{3,2,1,0:T(8,128)(2,1)} %get-tuple-element.400) | copy-start | bytes 2949124
  262.4 17.9 %collective-permute-start.42 = (bf16[96,1024]{1,0:T(8,128)(2,1)S(1)}, bf16[96,1024]{1,0:T(8,128)(2,1)S(1)}, u32[]{:S(2)}, u32[]{:S(2)}) collective-permute-start(bf16[96,1024]{1,0:T(8,128)(2,1)S(1)} %get-tuple-element.436), channel_id=1, source_target_pairs={{0,8},{1,9},{2,10},{3,11},{4,12},{5,13},{6,14},{7,15},{8,16},{9,17... | collective-permute-start | bytes 589832 | tf_op jit(solution)/shard_map/ppermute | solution.py:56
  280.7 8.9 %collective-permute-start.43 = (bf16[4,96,640]{2,1,0:T(8,128)(2,1)S(1)}, bf16[4,96,640]{2,1,0:T(8,128)(2,1)S(1)}, u32[]{:S(2)}, u32[]{:S(2)}) collective-permute-start(bf16[4,96,640]{2,1,0:T(8,128)(2,1)S(1)} %dynamic-slice_bitcast_fusion.4), channel_id=1, source_target_pairs={{0,4},{1,5},{2,3},{3,2},{4,0},{5,1},{6,7},{7,6},{8,12},{9,13},{10,... | collective-permute-start | bytes 1474568 | tf_op jit(solution)/shard_map/ppermute | solution.py:56
  281.8 1.5 collective-permute-start.44
  289.8 5.1 %collective-permute-start.45 = (bf16[96,640]{1,0:T(8,128)(2,1)S(1)}, bf16[96,640]{1,0:T(8,128)(2,1)S(1)}, u32[]{:S(2)}, u32[]{:S(2)}) collective-permute-start(bf16[96,640]{1,0:T(8,128)(2,1)S(1)} %get-tuple-element.444), channel_id=1, source_target_pairs={{0,24},{1,25},{2,26},{3,27},{4,28},{5,29},{6,30},{7,31},{8,0},{9,1... | collective-permute-start | bytes 368648 | tf_op jit(solution)/shard_map/ppermute | solution.py:56
  289.8 11.6 %collective-permute-start.46 = (bf16[96,640]{1,0:T(8,128)(2,1)S(1)}, bf16[96,640]{1,0:T(8,128)(2,1)S(1)}, u32[]{:S(2)}, u32[]{:S(2)}) collective-permute-start(bf16[96,640]{1,0:T(8,128)(2,1)S(1)} %get-tuple-element.446), channel_id=1, source_target_pairs={{0,16},{1,17},{2,18},{3,19},{4,20},{5,21},{6,22},{7,23},{8,24},{9,... | collective-permute-start | bytes 368648 | tf_op jit(solution)/shard_map/ppermute | solution.py:56
  291.2 10.2 %collective-permute-start.47 = (bf16[96,640]{1,0:T(8,128)(2,1)S(1)}, bf16[96,640]{1,0:T(8,128)(2,1)S(1)}, u32[]{:S(2)}, u32[]{:S(2)}) collective-permute-start(bf16[96,640]{1,0:T(8,128)(2,1)S(1)} %get-tuple-element.445), channel_id=1, source_target_pairs={{0,8},{1,9},{2,10},{3,11},{4,12},{5,13},{6,14},{7,15},{8,16},{9,17... | collective-permute-start | bytes 368648 | tf_op jit(solution)/shard_map/ppermute | solution.py:56
  301.6 1.5 collective-permute-start.48
  (9 other events, 11.3 us)
where the time goes:
time: 311 us; the launch traced here: 305 us
  Pallas kernels  164 us (53%)
  waiting for transfers between devices  60 us (19%)
  starting transfers between devices  43.1 us (14%)
  other arithmetic  20.5 us (7%)
  local copies, waits for them, and re-layouts  15.4 us (5%)
    ppermute x50, waiting for transfers between devices, send(): return lax.ppermute(value, AXES, route)  60 us
    ppermute x50, starting transfers between devices, send(): return lax.ppermute(value, AXES, route)  43.1 us
    pallas_call x3, Pallas kernels, weigh_call(): pl.pallas_call(functools.partial(weigh_kernel, plan), in_specs=[pl.BlockS...  41.1 us
    pallas_call x4, Pallas kernels, attend(): pl.pallas_call(functools.partial(attend_kernel, t, len(carry)), grid=(1,)...  33.6 us
    pallas_call x1, Pallas kernels, middle(): pl.pallas_call(middle_kernel, grid=(rows // BLOCK,), in_specs=set_specs()...  33.2 us
    pallas_call x2, Pallas kernels, attend_back(): pl.pallas_call(functools.partial(attend_back_kernel, t), grid=(seqs,), in...  25.8 us
    pallas_call x1, Pallas kernels, widen(): pl.pallas_call(widen_kernel, grid=(rows // BLOCK,), in_specs=set_specs()...  19.7 us
    pallas_call x1, Pallas kernels, input_back(): pl.pallas_call(input_kernel, grid=(rows // BLOCK,), in_specs=set_specs()...  10.5 us
  transfers between devices with their start and end apart: 50, of which 18 were waited for; matrix products, arithmetic and copies ran while one was open for 5% of the time, Pallas kernels for 54%

commit v1 on v0

--- a/solution.py
+++ b/solution.py
@@ -878,7 +878,10 @@
     two.go()
     three.go(2)
     input_grad = input_back(grad_resid_one, parts, weights_one)
-    input_grad = sync(one, two, input_grad)
+    if isinstance(two.value, list):
+        first, second, third = two.value
+        input_grad, first, third = sync(one, input_grad, first, third)
+        two.value = [first, second, third]
     one.go()
     one.go()
     two.go(2)

time: 311 us -> 307 us (0.987)
  waiting for transfers between devices: 60 us -> 53.9 us
    ppermute x50, waiting for transfers between devices: 60 us -> 53.9 us  [send(): return lax.ppermute(value, AXES, route)]
where the time goes in v1:
time: 307 us; the launch traced here: 301 us
  Pallas kernels  164 us (53%)
  waiting for transfers between devices  53.9 us (18%)
  starting transfers between devices  45.4 us (15%)
  other arithmetic  20.5 us (7%)
  local copies, waits for them, and re-layouts  15.4 us (5%)
    ppermute x50, waiting for transfers between devices, send(): return lax.ppermute(value, AXES, route)  53.9 us
    ppermute x50, starting transfers between devices, send(): return lax.ppermute(value, AXES, route)  45.4 us
    pallas_call x3, Pallas kernels, weigh_call(): pl.pallas_call(functools.partial(weigh_kernel, plan), in_specs=[pl.BlockS...  41.1 us
    pallas_call x4, Pallas kernels, attend(): pl.pallas_call(functools.partial(attend_kernel, t, len(carry)), grid=(1,)...  33.6 us
    pallas_call x1, Pallas kernels, middle(): pl.pallas_call(middle_kernel, grid=(rows // BLOCK,), in_specs=set_specs()...  33.2 us
    pallas_call x2, Pallas kernels, attend_back(): pl.pallas_call(functools.partial(attend_back_kernel, t), grid=(seqs,), in...  25.8 us
    pallas_call x1, Pallas kernels, widen(): pl.pallas_call(widen_kernel, grid=(rows // BLOCK,), in_specs=set_specs()...  19.7 us
    pallas_call x1, Pallas kernels, input_back(): pl.pallas_call(input_kernel, grid=(rows // BLOCK,), in_specs=set_specs()...  10.4 us
  transfers between devices with their start and end apart: 50, of which 18 were waited for; matrix products, arithmetic and copies ran while one was open for 5% of the time, Pallas kernels for 54%

profile of v1, /device:TPU:0, one launch (start us, length us, event | category | flops | bytes accessed | tf_op | source)
XLA Modules:
  0.0 301.2 jit_solution(10486956052585387462)
XLA Ops:
  0.7 1.0 copy.53
  3.0 0.9 collective-permute-done
  4.0 5.0 %collective-permute-start.1 = (bf16[96,640]{1,0:T(8,128)(2,1)S(1)}, bf16[96,640]{1,0:T(8,128)(2,1)S(1)}, u32[]{:S(2)}, u32[]{:S(2)}) collective-permute-start(bf16[96,640]{1,0:T(8,128)(2,1)S(1)} %maximum_select_fusion.9), channel_id=1, source_target_pairs={{0,24},{1,25},{2,26},{3,27},{4,28},{5,29},{6,30},{7,31},{8,0},{9,1... | collective-permute-start | bytes 368648 | tf_op jit(solution)/shard_map/ppermute | solution.py:56
  9.0 1.0 collective-permute-start.3
  10.0 0.9 fusion.14
  12.7 7.4 %collective-permute-done.2 = bf16[96,640]{1,0:T(8,128)(2,1)S(1)} collective-permute-done((bf16[96,640]{1,0:T(8,128)(2,1)S(1)}, bf16[96,640]{1,0:T(8,128)(2,1)S(1)}, u32[]{:S(2)}, u32[]{:S(2)}) %collective-permute-start.2) | collective-permute-done | bytes 122912 | tf_op jit(solution)/shard_map/ppermute | solution.py:56
  20.1 1.0 broadcast_in_dim.9.col_ref
  21.3 1.6 collective-permute-start.7
  23.3 7.5 %collective-permute-done.6 = bf16[96,1024]{1,0:T(8,128)(2,1)S(1)} collective-permute-done((bf16[96,1024]{1,0:T(8,128)(2,1)S(1)}, bf16[96,1024]{1,0:T(8,128)(2,1)S(1)}, u32[]{:S(2)}, u32[]{:S(2)}) %collective-permute-start.6) | collective-permute-done | bytes 196640 | tf_op jit(solution)/shard_map/ppermute | solution.py:56
  30.9 1.1 collective-permute-start.8
  32.1 2.2 collective-permute-start.10
  35.0 7.8 %collective-permute-done.10 = bf16[96,1024]{1,0:T(8,128)(2,1)S(1)} collective-permute-done((bf16[96,1024]{1,0:T(8,128)(2,1)S(1)}, bf16[96,1024]{1,0:T(8,128)(2,1)S(1)}, u32[]{:S(2)}, u32[]{:S(2)}) %collective-permute-start.10) | collective-permute-done | bytes 196640 | tf_op jit(solution)/shard_map/ppermute | solution.py:56
  43.2 2.0 collective-permute-done.8
  45.4 1.9 maximum_select_fusion.2.mine_ref
  47.4 1.6 collective-permute-start.11
  48.9 2.4 collective-permute-done.12.other_ref
  51.3 1.3 copy-done.2
  52.6 8.4 %attend.4 = (bf16[1,1024,640]{2,1,0:T(8,128)(2,1)}, bf16[1,1024,512]{2,1,0:T(8,128)(2,1)}, bf16[2,3,512,1024]{3,2,1,0:T(8,128)(2,1)}, bf16[2,1024,256]{2,1,0:T(8...) custom-call(s32[1]{0:T(128)} %bitcast.22.side_ref.side_two_ref, ...), custom_call_target="tpu_custom_call" | custom-call | flops 100000000 | bytes 100000 | tf_op jit(solution)/shard_map/attend/pallas_call | solution.py:322
  61.3 1.1 collective-permute-start.13
  62.4 2.6 collective-permute-start.14
  65.0 0.8 collective-permute-start.15
  65.8 1.1 collective-permute-start.16
  67.0 8.5 %attend.5 = (bf16[1,1024,640]{2,1,0:T(8,128)(2,1)}, bf16[1,1024,512]{2,1,0:T(8,128)(2,1)}, bf16[2,3,512,1024]{3,2,1,0:T(8,128)(2,1)}, bf16[2,1024,256]{2,1,0:T(8...) custom-call(s32[1]{0:T(128)} %bitcast.22.side_ref.side_two_ref, ...), custom_call_target="tpu_custom_call", output_to_operand_aliasing={{0}: (6, {}), {1}: (7, {}), {2}: (8, {}), {3}: (9, {}), {4}... | custom-call | flops 100000000 | bytes 100000 | tf_op jit(solution)/shard_map/attend/pallas_call | solution.py:322
  75.5 8.3 %attend.6 = (bf16[1,1024,640]{2,1,0:T(8,128)(2,1)}, bf16[1,1024,512]{2,1,0:T(8,128)(2,1)}, bf16[2,3,512,1024]{3,2,1,0:T(8,128)(2,1)}, bf16[2,1024,256]{2,1,0:T(8...) custom-call(s32[1]{0:T(128)} %bitcast.22.side_ref.side_two_ref, ...), custom_call_target="tpu_custom_call" | custom-call | flops 100000000 | bytes 100000 | tf_op jit(solution)/shard_map/attend/pallas_call | solution.py:322
  84.1 0.9 constant_dynamic-slice_fusion
  84.9 1.0 maximum_select_fusion.mine_ref.mine_two_ref
  86.0 1.5 collective-permute-start.18
  87.6 1.1 fusion.9
  89.4 8.3 %attend.7 = (bf16[1,1024,640]{2,1,0:T(8,128)(2,1)}, bf16[1,1024,512]{2,1,0:T(8,128)(2,1)}, bf16[2,3,512,1024]{3,2,1,0:T(8,128)(2,1)}, bf16[2,1024,256]{2,1,0:T(8...) custom-call(s32[1]{0:T(128)} %bitcast.22.side_ref.side_two_ref, ...), custom_call_target="tpu_custom_call", output_to_operand_aliasing={{0}: (6, {}), {1}: (7, {}), {2}: (8, {}), {3}: (9, {}), {4}... | custom-call | flops 100000000 | bytes 100000 | tf_op jit(solution)/shard_map/attend/pallas_call | solution.py:322
  97.8 1.9 maximum_select_fusion.4
  100.3 1.1 dynamic-slice_bitcast_fusion.3
  102.0 19.7 %widen.1 = (f32[1024,768]{1,0:T(8,128)}, bf16[768,1024]{1,0:T(8,128)(2,1)}, bf16[768,1024]{1,0:T(8,128)(2,1)}, bf16[1024,1536]{1,0:T(8,128)(2,1)}, bf16[1024,153...) custom-call(s32[1]{0:T(128)} %bitcast.22.side_ref.side_two_ref, ...), custom_call_target="tpu_custom_call" | custom-call | flops 100000000 | bytes 100000 | tf_op jit(solution)/shard_map/widen/pallas_call | solution.py:500
  121.8 0.8 copy-done.17
  123.0 2.0 maximum_select_fusion.1.mine_ref
  125.1 4.5 %collective-permute-done.22.other_ref = bf16[2,2,4,96,768]{4,3,2,1,0:T(8,128)(2,1)S(1)} collective-permute-done((bf16[2,2,4,96,768]{4,3,2,1,0:T(8,128)(2,1)S(1)}, bf16[2,2,4,96,768]{4,3,2,1,0:T(8,128)(2,1)S(1)}, u32[]{:S(2)}, u32[]{:S(2)}) %collective-permute-start.22) | collective-permute-done | bytes 2359328 | tf_op jit(solution)/shard_map/ppermute | solution.py:56
  131.0 33.2 %middle.1 = (bf16[1024,768]{1,0:T(8,128)(2,1)}, bf16[768,1024]{1,0:T(8,128)(2,1)}, bf16[1024,1536]{1,0:T(8,128)(2,1)}, bf16[1024,1536]{1,0:T(8,128)(2,1)}, f32[1...) custom-call(s32[1]{0:T(128)} %bitcast.22.side_ref.side_two_ref, ...), custom_call_target="tpu_custom_call" | custom-call | flops 100000000 | bytes 100000 | tf_op jit(solution)/shard_map/middle/pallas_call | solution.py:578
  164.5 3.5 %collective-permute-done.26.refs_1_ = bf16[768,1024]{1,0:T(8,128)(2,1)S(1)} collective-permute-done((bf16[768,1024]{1,0:T(8,128)(2,1)}, bf16[768,1024]{1,0:T(8,128)(2,1)S(1)}, u32[]{:S(2)}, u32[]{:S(2)}) %collective-permute-start.26) | collective-permute-done | bytes 1572896 | tf_op jit(solution)/shard_map/ppermute | solution.py:56
  168.0 1.2 copy-done.9
  171.0 12.2 %weigh.3 = (bf16[2,4,96,768]{3,2,1,0:T(8,128)(2,1)}, bf16[2,4,96,768]{3,2,1,0:T(8,128)(2,1)}) custom-call(s32[2]{0:T(128)} %pad_add_fusion.place_ref, f32[8,128]{1,0:T(8,128)} %broadcast_1_stats_ref_stats_got_ref.2.stats_ref.stats_got_ref, f32[8,128]{1,0:T(8,128)} %broadcast_1_stats_ref_stats_got_ref.2.stats_ref.stats_got_ref, ...), custom_call_target="tpu_custom_call" | custom-call | flops 100000000 | bytes 100000 | tf_op jit(solution)/shard_map/weigh/pallas_call | solution.py:670
  183.3 1.2 copy-done.8
  184.5 1.5 collective-permute-start.31
  186.1 15.9 %weigh.4 = (bf16[2,4,96,1024]{3,2,1,0:T(8,128)(2,1)}, bf16[2,4,96,1024]{3,2,1,0:T(8,128)(2,1)}) custom-call(s32[2]{0:T(128)} %pad_add_fusion.place_ref, f32[8,128]{1,0:T(8,128)} %broadcast_1_stats_ref_stats_got_ref.2.stats_ref.stats_got_ref, f32[8,128]{1,0:T(8,128)} %broadcast_1_stats_ref_stats_got_ref.2.stats_ref.stats_got_ref, ...), custom_call_target="tpu_custom_call" | custom-call | flops 100000000 | bytes 100000 | tf_op jit(solution)/shard_map/weigh/pallas_call | solution.py:670
  202.1 1.6 collective-permute-start.30
  203.7 13.0 %attend_back.2 = (bf16[1024,640]{1,0:T(8,128)(2,1)}, bf16[1024,640]{1,0:T(8,128)(2,1)}) custom-call(s32[1]{0:T(128)} %bitcast.22.side_ref.side_two_ref, bf16[2,2,4,96,1024]{4,3,2,1,0:T(8,128)(2,1)} %copy-done, bf16[2,2,4,96,1024]{4,3,2,1,0:T(8,128)(2,1)} %collective-permute-done.17.other_ref.other_two_ref, bf16[1024,768]{1,0:T(8,128)(2,1)} %get-tuple-element.368.g_ref, ...), custom_call_target="tpu_custom_call" | custom-call | flops 100000000 | bytes 100000 | tf_op jit(solution)/shard_map/attend_back/pallas_call | solution.py:423
  216.7 1.7 add_convert_fusion.1
  218.5 1.0 collective-permute-start.32
  219.5 12.9 %attend_back.3 = (bf16[1024,640]{1,0:T(8,128)(2,1)}, bf16[1024,640]{1,0:T(8,128)(2,1)}) custom-call(s32[1]{0:T(128)} %bitcast.22.side_ref.side_two_ref, bf16[2,2,4,96,1024]{4,3,2,1,0:T(8,128)(2,1)} %copy-done, bf16[2,2,4,96,1024]{4,3,2,1,0:T(8,128)(2,1)} %collective-permute-done.17.other_ref.other_two_ref, bf16[1024,768]{1,0:T(8,128)(2,1)} %get-tuple-element.368.g_ref, ...), custom_call_target="tpu_custom_call" | custom-call | flops 100000000 | bytes 100000 | tf_op jit(solution)/shard_map/attend_back/pallas_call | solution.py:423
  232.4 0.8 copy-done.15
  233.2 1.6 fusion.1
  235.6 2.6 add_convert_fusion
  238.2 1.0 dynamic-slice_bitcast_fusion
  239.2 1.1 collective-permute-start.35
  240.3 2.4 collective-permute-start.36
  243.3 12.9 %weigh.5 = (bf16[2,4,96,640]{3,2,1,0:T(8,128)(2,1)}, bf16[2,4,96,640]{3,2,1,0:T(8,128)(2,1)}) custom-call(s32[2]{0:T(128)} %pad_add_fusion.place_ref, f32[768,128]{1,0:T(8,128)} %get-tuple-element.328.stats_ref, f32[768,128]{1,0:T(8,128)} %copy-done.18, bf16[768,1024]{1,0:T(8,128)(2,1)} %get-tuple-element.320.refs_0_, ...), custom_call_target="tpu_custom_call" | custom-call | flops 100000000 | bytes 100000 | tf_op jit(solution)/shard_map/weigh/pallas_call | solution.py:670
  256.4 1.1 collective-permute-start.39
  258.0 3.6 %collective-permute-start.40 = (bf16[96,1024]{1,0:T(8,128)(2,1)S(1)}, bf16[96,1024]{1,0:T(8,128)(2,1)S(1)}, u32[]{:S(2)}, u32[]{:S(2)}) collective-permute-start(bf16[96,1024]{1,0:T(8,128)(2,1)S(1)} %get-tuple-element.436), channel_id=1, source_target_pairs={{0,24},{1,25},{2,26},{3,27},{4,28},{5,29},{6,30},{7,31},{8,0},{9,1... | collective-permute-start | bytes 589832 | tf_op jit(solution)/shard_map/ppermute | solution.py:56
  261.6 0.8 collective-permute-start.43
  262.4 10.4 %input_back.1 = bf16[1024,768]{1,0:T(8,128)(2,1)} custom-call(s32[1]{0:T(128)} %bitcast.22.side_ref.side_two_ref, bf16[2,2,4,96,640]{4,3,2,1,0:T(8,128)(2,1)} %copy-done.1, bf16[2,2,4,96,640]{4,3,2,1,0:T(8,128)(2,1)} %copy-done.2, f32[1024,768]{1,0:T(8,128)} %get-tuple-element.394.res_ref, bf16[1024,640]{1,0:T(8,128)(2,1)} %get-tuple-element.383.refs_2_.um_ref, ...), custom_call_target="tpu_custom_call" | custom-call | flops 100000000 | bytes 100000 | tf_op jit(solution)/shard_map/input_back/pallas_call | solution.py:732
  273.2 1.0 collective-permute-start.42
  274.3 6.1 %collective-permute-done.43 = bf16[96,1024]{1,0:T(8,128)(2,1)S(1)} collective-permute-done((bf16[96,1024]{1,0:T(8,128)(2,1)S(1)}, bf16[96,1024]{1,0:T(8,128)(2,1)S(1)}, u32[]{:S(2)}, u32[]{:S(2)}) %collective-permute-start.43) | collective-permute-done | bytes 196640 | tf_op jit(solution)/shard_map/ppermute | solution.py:56
  282.3 3.2 %collective-permute-start.45 = (bf16[96,640]{1,0:T(8,128)(2,1)S(1)}, bf16[96,640]{1,0:T(8,128)(2,1)S(1)}, u32[]{:S(2)}, u32[]{:S(2)}) collective-permute-start(bf16[96,640]{1,0:T(8,128)(2,1)S(1)} %get-tuple-element.442), channel_id=1, source_target_pairs={{0,24},{1,25},{2,26},{3,27},{4,28},{5,29},{6,30},{7,31},{8,0},{9,1... | collective-permute-start | bytes 368648 | tf_op jit(solution)/shard_map/ppermute | solution.py:56
  285.5 2.5 collective-permute-start.46
  288.1 1.6 collective-permute-done.45
  289.7 7.9 %collective-permute-done.46 = bf16[96,640]{1,0:T(8,128)(2,1)S(1)} collective-permute-done((bf16[96,640]{1,0:T(8,128)(2,1)S(1)}, bf16[96,640]{1,0:T(8,128)(2,1)S(1)}, u32[]{:S(2)}, u32[]{:S(2)}) %collective-permute-start.46) | collective-permute-done | bytes 122912 | tf_op jit(solution)/shard_map/ppermute | solution.py:56
  (180 shorter events, 19.4 us)
Async XLA Ops:
  0.6 11.0 %copy-start.22 = (s32[2048]{0:T(1024)S(1)}, s32[2048]{0:T(1024)}, u32[]{:S(2)}) copy-start(s32[2048]{0:T(1024)} %param.12) | copy-start | bytes 24580
  0.7 10.4 %copy-start.21 = (bf16[384,48]{0,1:T(8,128)(2,1)S(1)}, bf16[384,48]{0,1:T(8,128)(2,1)}, u32[]{:S(2)}) copy-start(bf16[384,48]{0,1:T(8,128)(2,1)} %param.14) | copy-start | bytes 110596
  0.7 10.4 %copy-start.19 = (bf16[48,1536]{1,0:T(8,128)(2,1)S(1)}, bf16[48,1536]{1,0:T(8,128)(2,1)}, u32[]{:S(2)}) copy-start(bf16[48,1536]{1,0:T(8,128)(2,1)} %param.15) | copy-start | bytes 442372
  2.5 1.4 collective-permute-start
  4.0 8.7 %collective-permute-start.1 = (bf16[96,640]{1,0:T(8,128)(2,1)S(1)}, bf16[96,640]{1,0:T(8,128)(2,1)S(1)}, u32[]{:S(2)}, u32[]{:S(2)}) collective-permute-start(bf16[96,640]{1,0:T(8,128)(2,1)S(1)} %maximum_select_fusion.9), channel_id=1, source_target_pairs={{0,24},{1,25},{2,26},{3,27},{4,28},{5,29},{6,30},{7,31},{8,0},{9,1... | collective-permute-start | bytes 368648 | tf_op jit(solution)/shard_map/ppermute | solution.py:56
  9.0 11.1 %collective-permute-start.2 = (bf16[96,640]{1,0:T(8,128)(2,1)S(1)}, bf16[96,640]{1,0:T(8,128)(2,1)S(1)}, u32[]{:S(2)}, u32[]{:S(2)}) collective-permute-start(bf16[96,640]{1,0:T(8,128)(2,1)S(1)} %maximum_select_fusion.9), channel_id=1, source_target_pairs={{0,16},{1,17},{2,18},{3,19},{4,20},{5,21},{6,22},{7,23},{8,24},{9,... | collective-permute-start | bytes 368648 | tf_op jit(solution)/shard_map/ppermute | solution.py:56
  9.0 11.1 %collective-permute-start.3 = (bf16[96,640]{1,0:T(8,128)(2,1)S(1)}, bf16[96,640]{1,0:T(8,128)(2,1)S(1)}, u32[]{:S(2)}, u32[]{:S(2)}) collective-permute-start(bf16[96,640]{1,0:T(8,128)(2,1)S(1)} %maximum_select_fusion.9), channel_id=1, source_target_pairs={{0,8},{1,9},{2,10},{3,11},{4,12},{5,13},{6,14},{7,15},{8,16},{9,17... | collective-permute-start | bytes 368648 | tf_op jit(solution)/shard_map/ppermute | solution.py:56
  10.9 1.3 collective-permute-start.5
  11.1 1.5 collective-permute-start.4
  11.7 9.6 %copy-start.20 = (s32[1024]{0:T(1024)}, s32[1024]{0:T(1024)S(1)}, u32[]{:S(2)}) copy-start(s32[1024]{0:T(1024)S(1)} %dynamic_slice.100) | copy-start | bytes 12292
  21.3 9.5 %collective-permute-start.7 = (bf16[4,96,640]{2,1,0:T(8,128)(2,1)S(1)}, bf16[4,96,640]{2,1,0:T(8,128)(2,1)S(1)}, u32[]{:S(2)}, u32[]{:S(2)}) collective-permute-start(bf16[4,96,640]{2,1,0:T(8,128)(2,1)S(1)} %constant_dynamic-slice_fusion.2), channel_id=1, source_target_pairs={{0,4},{1,5},{2,3},{3,2},{4,0},{5,1},{6,7},{7,6},{8,12},{9,13},{10,... | collective-permute-start | bytes 1474568 | tf_op jit(solution)/shard_map/ppermute | solution.py:56
  22.8 7.9 %collective-permute-start.6 = (bf16[96,1024]{1,0:T(8,128)(2,1)S(1)}, bf16[96,1024]{1,0:T(8,128)(2,1)S(1)}, u32[]{:S(2)}, u32[]{:S(2)}) collective-permute-start(bf16[96,1024]{1,0:T(8,128)(2,1)S(1)} %maximum_select_fusion.7), channel_id=1, source_target_pairs={{0,8},{1,9},{2,10},{3,11},{4,12},{5,13},{6,14},{7,15},{8,16},{9,17... | collective-permute-start | bytes 589832 | tf_op jit(solution)/shard_map/ppermute | solution.py:56
  30.9 14.3 %collective-permute-start.8 = (bf16[2,4,96,640]{3,2,1,0:T(8,128)(2,1)S(1)}, bf16[2,4,96,640]{3,2,1,0:T(8,128)(2,1)}, u32[]{:S(2)}, u32[]{:S(2)}) collective-permute-start(bf16[2,4,96,640]{3,2,1,0:T(8,128)(2,1)S(1)} %maximum_select_fusion.6), channel_id=1, source_target_pairs={{0,1},{1,0},{2,6},{3,7},{4,5},{5,4},{6,2},{7,3},{8,9},{9,8},{10,14... | collective-permute-start | bytes 2949128 | tf_op jit(solution)/shard_map/ppermute | solution.py:56
  32.1 10.7 %collective-permute-start.10 = (bf16[96,1024]{1,0:T(8,128)(2,1)S(1)}, bf16[96,1024]{1,0:T(8,128)(2,1)S(1)}, u32[]{:S(2)}, u32[]{:S(2)}) collective-permute-start(bf16[96,1024]{1,0:T(8,128)(2,1)S(1)} %maximum_select_fusion.7), channel_id=1, source_target_pairs={{0,16},{1,17},{2,18},{3,19},{4,20},{5,21},{6,22},{7,23},{8,24},{9,... | collective-permute-start | bytes 589832 | tf_op jit(solution)/shard_map/ppermute | solution.py:56
  34.3 8.9 %collective-permute-start.9 = (bf16[96,1024]{1,0:T(8,128)(2,1)S(1)}, bf16[96,1024]{1,0:T(8,128)(2,1)S(1)}, u32[]{:S(2)}, u32[]{:S(2)}) collective-permute-start(bf16[96,1024]{1,0:T(8,128)(2,1)S(1)} %maximum_select_fusion.7), channel_id=1, source_target_pairs={{0,24},{1,25},{2,26},{3,27},{4,28},{5,29},{6,30},{7,31},{8,0},{9,1... | collective-permute-start | bytes 589832 | tf_op jit(solution)/shard_map/ppermute | solution.py:56
  47.3 4.1 %copy-start.1 = (bf16[2,2,4,96,640]{4,3,2,1,0:T(8,128)(2,1)}, bf16[2,2,4,96,640]{4,3,2,1,0:T(8,128)(2,1)S(1)}, u32[]{:S(2)}) copy-start(bf16[2,2,4,96,640]{4,3,2,1,0:T(8,128)(2,1)S(1)} %maximum_select_fusion.2.mine_ref) | copy-start | bytes 5898244
  47.3 4.0 %collective-permute-start.12 = (bf16[2,2,4,96,640]{4,3,2,1,0:T(8,128)(2,1)S(1)}, bf16[2,2,4,96,640]{4,3,2,1,0:T(8,128)(2,1)S(1)}, u32[]{:S(2)}, u32[]{:S(2)}) collective-permute-start(bf16[2,2,4,96,640]{4,3,2,1,0:T(8,128)(2,1)S(1)} %maximum_select_fusion.2.mine_ref), channel_id=1, source_target_pairs={{0,2},{1,3},{2,0},{3,1},{4,6},{5,7},{6,4},{7,5},{8,10},{9,11},{10,... | collective-permute-start | bytes 5898248 | tf_op jit(solution)/shard_map/ppermute | solution.py:56
  47.4 13.6 %collective-permute-start.11 = (bf16[4,96,1024]{2,1,0:T(8,128)(2,1)S(1)}, bf16[4,96,1024]{2,1,0:T(8,128)(2,1)S(1)}, u32[]{:S(2)}, u32[]{:S(2)}) collective-permute-start(bf16[4,96,1024]{2,1,0:T(8,128)(2,1)S(1)} %constant_dynamic-slice_fusion.1), channel_id=1, source_target_pairs={{0,4},{1,5},{2,3},{3,2},{4,0},{5,1},{6,7},{7,6},{8,12},{9,13},{10,... | collective-permute-start | bytes 2359304 | tf_op jit(solution)/shard_map/ppermute | solution.py:56
  61.3 22.6 %collective-permute-start.13 = (bf16[2,4,96,1024]{3,2,1,0:T(8,128)(2,1)S(1)}, bf16[2,4,96,1024]{3,2,1,0:T(8,128)(2,1)S(1)}, u32[]{:S(2)}, u32[]{:S(2)}) collective-permute-start(bf16[2,4,96,1024]{3,2,1,0:T(8,128)(2,1)S(1)} %maximum_select_fusion.3), channel_id=1, source_target_pairs={{0,1},{1,0},{2,6},{3,7},{4,5},{5,4},{6,2},{7,3},{8,9},{9,8},{10,14... | collective-permute-start | bytes 4718600 | tf_op jit(solution)/shard_map/ppermute | solution.py:56
  62.4 21.5 %collective-permute-start.14 = (bf16[96,768]{1,0:T(8,128)(2,1)S(1)}, bf16[96,768]{1,0:T(8,128)(2,1)S(1)}, u32[]{:S(2)}, u32[]{:S(2)}) collective-permute-start(bf16[96,768]{1,0:T(8,128)(2,1)S(1)} %maximum_select_fusion.8), channel_id=1, source_target_pairs={{0,24},{1,25},{2,26},{3,27},{4,28},{5,29},{6,30},{7,31},{8,0},{9,1... | collective-permute-start | bytes 442376 | tf_op jit(solution)/shard_map/ppermute | solution.py:56
  65.0 18.9 %collective-permute-start.15 = (bf16[96,768]{1,0:T(8,128)(2,1)S(1)}, bf16[96,768]{1,0:T(8,128)(2,1)S(1)}, u32[]{:S(2)}, u32[]{:S(2)}) collective-permute-start(bf16[96,768]{1,0:T(8,128)(2,1)S(1)} %maximum_select_fusion.8), channel_id=1, source_target_pairs={{0,16},{1,17},{2,18},{3,19},{4,20},{5,21},{6,22},{7,23},{8,24},{9,... | collective-permute-start | bytes 442376 | tf_op jit(solution)/shard_map/ppermute | solution.py:56
  65.8 18.1 %collective-permute-start.16 = (bf16[96,768]{1,0:T(8,128)(2,1)S(1)}, bf16[96,768]{1,0:T(8,128)(2,1)S(1)}, u32[]{:S(2)}, u32[]{:S(2)}) collective-permute-start(bf16[96,768]{1,0:T(8,128)(2,1)S(1)} %maximum_select_fusion.8), channel_id=1, source_target_pairs={{0,8},{1,9},{2,10},{3,11},{4,12},{5,13},{6,14},{7,15},{8,16},{9,17... | collective-permute-start | bytes 442376 | tf_op jit(solution)/shard_map/ppermute | solution.py:56
  86.0 11.8 %copy-start = (bf16[2,2,4,96,1024]{4,3,2,1,0:T(8,128)(2,1)}, bf16[2,2,4,96,1024]{4,3,2,1,0:T(8,128)(2,1)S(1)}, u32[]{:S(2)}) copy-start(bf16[2,2,4,96,1024]{4,3,2,1,0:T(8,128)(2,1)S(1)} %maximum_select_fusion.mine_ref.mine_two_ref) | copy-start | bytes 9437188
  86.0 11.8 %collective-permute-start.17 = (bf16[2,2,4,96,1024]{4,3,2,1,0:T(8,128)(2,1)S(1)}, bf16[2,2,4,96,1024]{4,3,2,1,0:T(8,128)(2,1)}, u32[]{:S(2)}, u32[]{:S(2)}) collective-permute-start(bf16[2,2,4,96,1024]{4,3,2,1,0:T(8,128)(2,1)S(1)} %maximum_select_fusion.mine_ref.mine_two_ref), channel_id=1, source_target_pairs={{0,2},{1,3},{2,0},{3,1},{4,6},{5,7},{6,4},{7,5},{8,10},{9,11},{10,... | collective-permute-start | bytes 9437192 | tf_op jit(solution)/shard_map/ppermute | solution.py:56
  86.0 11.7 %collective-permute-start.18 = (bf16[4,96,768]{2,1,0:T(8,128)(2,1)}, bf16[4,96,768]{2,1,0:T(8,128)(2,1)}, u32[]{:S(2)}, u32[]{:S(2)}) collective-permute-start(bf16[4,96,768]{2,1,0:T(8,128)(2,1)} %constant_dynamic-slice_fusion), channel_id=1, source_target_pairs={{0,4},{1,5},{2,3},{3,2},{4,0},{5,1},{6,7},{7,6},{8,12},{9,13},{10,... | collective-permute-start | bytes 1769480 | tf_op jit(solution)/shard_map/ppermute | solution.py:56
  97.8 3.6 %copy-start.3 = (bf16[2,1024,256]{2,1,0:T(8,128)(2,1)S(1)}, bf16[2,1024,256]{2,1,0:T(8,128)(2,1)}, u32[]{:S(2)}) copy-start(bf16[2,1024,256]{2,1,0:T(8,128)(2,1)} %get-tuple-element.298.v_ref.refs_4_) | copy-start | bytes 3145732
  99.7 22.1 %collective-permute-start.19 = (bf16[2,4,96,768]{3,2,1,0:T(8,128)(2,1)S(1)}, bf16[2,4,96,768]{3,2,1,0:T(8,128)(2,1)S(1)}, u32[]{:S(2)}, u32[]{:S(2)}) collective-permute-start(bf16[2,4,96,768]{3,2,1,0:T(8,128)(2,1)S(1)} %maximum_select_fusion.4), channel_id=1, source_target_pairs={{0,1},{1,0},{2,6},{3,7},{4,5},{5,4},{6,2},{7,3},{8,9},{9,8},{10,14... | collective-permute-start | bytes 3538952 | tf_op jit(solution)/shard_map/ppermute | solution.py:56
  101.4 20.4 %collective-permute-start.20 = (bf16[1024,256]{1,0:T(8,128)(2,1)S(1)}, bf16[1024,256]{1,0:T(8,128)(2,1)S(1)}, u32[]{:S(2)}, u32[]{:S(2)}) collective-permute-start(bf16[1024,256]{1,0:T(8,128)(2,1)S(1)} %dynamic-slice_bitcast_fusion.3), channel_id=1, source_target_pairs={{0,2},{1,3},{2,0},{3,1},{4,6},{5,7},{6,4},{7,5},{8,10},{9,11},{10,... | collective-permute-start | bytes 1572872 | tf_op jit(solution)/shard_map/ppermute | solution.py:56
  101.5 20.3 %collective-permute-start.21 = (bf16[1024,256]{1,0:T(8,128)(2,1)S(1)}, bf16[1024,256]{1,0:T(8,128)(2,1)S(1)}, u32[]{:S(2)}, u32[]{:S(2)}) collective-permute-start(bf16[1024,256]{1,0:T(8,128)(2,1)S(1)} %dynamic-slice_bitcast_fusion.2), channel_id=1, source_target_pairs={{0,2},{1,3},{2,0},{3,1},{4,6},{5,7},{6,4},{7,5},{8,10},{9,11},{10,... | collective-permute-start | bytes 1572872 | tf_op jit(solution)/shard_map/ppermute | solution.py:56
  121.8 3.3 %copy-start.16 = (bf16[1024,256]{1,0:T(8,128)(2,1)}, bf16[1024,256]{1,0:T(8,128)(2,1)S(1)}, u32[]{:S(2)}) copy-start(bf16[1024,256]{1,0:T(8,128)(2,1)S(1)} %collective-permute-done.20.refs_3_) | copy-start | bytes 1572868
  125.0 5.3 %copy-start.6 = (bf16[2,2,4,96,768]{4,3,2,1,0:T(8,128)(2,1)}, bf16[2,2,4,96,768]{4,3,2,1,0:T(8,128)(2,1)S(1)}, u32[]{:S(2)}) copy-start(bf16[2,2,4,96,768]{4,3,2,1,0:T(8,128)(2,1)S(1)} %maximum_select_fusion.1.mine_ref) | copy-start | bytes 7077892
  125.0 4.6 %collective-permute-start.22 = (bf16[2,2,4,96,768]{4,3,2,1,0:T(8,128)(2,1)S(1)}, bf16[2,2,4,96,768]{4,3,2,1,0:T(8,128)(2,1)S(1)}, u32[]{:S(2)}, u32[]{:S(2)}) collective-permute-start(bf16[2,2,4,96,768]{4,3,2,1,0:T(8,128)(2,1)S(1)} %maximum_select_fusion.1.mine_ref), channel_id=1, source_target_pairs={{0,2},{1,3},{2,0},{3,1},{4,6},{5,7},{6,4},{7,5},{8,10},{9,11},{10,... | collective-permute-start | bytes 7077896 | tf_op jit(solution)/shard_map/ppermute | solution.py:56
  129.6 34.7 %collective-permute-start.23 = (bf16[1024,1536]{1,0:T(8,128)(2,1)}, bf16[1024,1536]{1,0:T(8,128)(2,1)S(1)}, u32[]{:S(2)}, u32[]{:S(2)}) collective-permute-start(bf16[1024,1536]{1,0:T(8,128)(2,1)} %get-tuple-element.318.ho_ref), channel_id=1, source_target_pairs={{0,2},{1,3},{2,0},{3,1},{4,6},{5,7},{6,4},{7,5},{8,10},{9,11},{10,... | collective-permute-start | bytes 9437192 | tf_op jit(solution)/shard_map/ppermute | solution.py:56
  129.7 34.5 %collective-permute-start.24 = (bf16[768,1024]{1,0:T(8,128)(2,1)}, bf16[768,1024]{1,0:T(8,128)(2,1)}, u32[]{:S(2)}, u32[]{:S(2)}) collective-permute-start(bf16[768,1024]{1,0:T(8,128)(2,1)} %get-tuple-element.319.refs_6_), channel_id=1, source_target_pairs={{0,2},{1,3},{2,0},{3,1},{4,6},{5,7},{6,4},{7,5},{8,10},{9,11},{10,... | collective-permute-start | bytes 4718600 | tf_op jit(solution)/shard_map/ppermute | solution.py:56
  130.1 34.2 %collective-permute-start.25 = (bf16[768,1024]{1,0:T(8,128)(2,1)}, bf16[768,1024]{1,0:T(8,128)(2,1)}, u32[]{:S(2)}, u32[]{:S(2)}) collective-permute-start(bf16[768,1024]{1,0:T(8,128)(2,1)} %get-tuple-element.320.refs_0_), channel_id=1, source_target_pairs={{0,2},{1,3},{2,0},{3,1},{4,6},{5,7},{6,4},{7,5},{8,10},{9,11},{10,... | collective-permute-start | bytes 4718600 | tf_op jit(solution)/shard_map/ppermute | solution.py:56
  164.3 6.7 %copy-start.4 = (bf16[1024,1536]{1,0:T(8,128)(2,1)}, bf16[1024,1536]{1,0:T(8,128)(2,1)S(1)}, u32[]{:S(2)}) copy-start(bf16[1024,1536]{1,0:T(8,128)(2,1)S(1)} %collective-permute-done.23.refs_3_.refs_5_) | copy-start | bytes 9437188
  164.3 3.7 %collective-permute-start.26 = (bf16[768,1024]{1,0:T(8,128)(2,1)}, bf16[768,1024]{1,0:T(8,128)(2,1)S(1)}, u32[]{:S(2)}, u32[]{:S(2)}) collective-permute-start(bf16[768,1024]{1,0:T(8,128)(2,1)} %get-tuple-element.324.refs_0_), channel_id=1, source_target_pairs={{0,2},{1,3},{2,0},{3,1},{4,6},{5,7},{6,4},{7,5},{8,10},{9,11},{10,... | collective-permute-start | bytes 4718600 | tf_op jit(solution)/shard_map/ppermute | solution.py:56
  169.2 14.1 %collective-permute-start.27 = (bf16[1024,1536]{1,0:T(8,128)(2,1)}, bf16[1024,1536]{1,0:T(8,128)(2,1)S(1)}, u32[]{:S(2)}, u32[]{:S(2)}) collective-permute-start(bf16[1024,1536]{1,0:T(8,128)(2,1)} %get-tuple-element.333), channel_id=1, source_target_pairs={{0,2},{1,3},{2,0},{3,1},{4,6},{5,7},{6,4},{7,5},{8,10},{9,11},{10,... | collective-permute-start | bytes 9437192 | tf_op jit(solution)/shard_map/ppermute | solution.py:56
  169.3 14.0 %collective-permute-start.28 = (bf16[768,1024]{1,0:T(8,128)(2,1)}, bf16[768,1024]{1,0:T(8,128)(2,1)S(1)}, u32[]{:S(2)}, u32[]{:S(2)}) collective-permute-start(bf16[768,1024]{1,0:T(8,128)(2,1)} %get-tuple-element.334.refs_0_), channel_id=1, source_target_pairs={{0,2},{1,3},{2,0},{3,1},{4,6},{5,7},{6,4},{7,5},{8,10},{9,11},{10,... | collective-permute-start | bytes 4718600 | tf_op jit(solution)/shard_map/ppermute | solution.py:56
  169.7 13.6 %collective-permute-start.29 = (f32[768,128]{1,0:T(8,128)}, f32[768,128]{1,0:T(8,128)S(1)}, u32[]{:S(2)}, u32[]{:S(2)}) collective-permute-start(f32[768,128]{1,0:T(8,128)} %get-tuple-element.328.stats_ref), channel_id=1, source_target_pairs={{0,2},{1,3},{2,0},{3,1},{4,6},{5,7},{6,4},{7,5},{8,10},{9,11},{10,... | collective-permute-start | bytes 1179656 | tf_op jit(solution)/shard_map/ppermute | solution.py:56
  183.3 18.8 %copy-start.18 = (f32[768,128]{1,0:T(8,128)}, f32[768,128]{1,0:T(8,128)S(1)}, u32[]{:S(2)}) copy-start(f32[768,128]{1,0:T(8,128)S(1)} %collective-permute-done.29.stats_got_ref) | copy-start | bytes 1179652
  184.5 32.1 %collective-permute-start.31 = (bf16[2,4,96,768]{3,2,1,0:T(8,128)(2,1)}, bf16[2,4,96,768]{3,2,1,0:T(8,128)(2,1)}, u32[]{:S(2)}, u32[]{:S(2)}) collective-permute-start(bf16[2,4,96,768]{3,2,1,0:T(8,128)(2,1)} %get-tuple-element.348), channel_id=1, source_target_pairs={{0,1},{1,0},{2,6},{3,7},{4,5},{5,4},{6,2},{7,3},{8,9},{9,8},{10,14... | collective-permute-start | bytes 3538952 | tf_op jit(solution)/shard_map/ppermute | solution.py:56
  202.1 14.6 %copy-start.12 = (bf16[2,4,96,768]{3,2,1,0:T(8,128)(2,1)S(1)}, bf16[2,4,96,768]{3,2,1,0:T(8,128)(2,1)}, u32[]{:S(2)}) copy-start(bf16[2,4,96,768]{3,2,1,0:T(8,128)(2,1)} %get-tuple-element.347) | copy-start | bytes 3538948
  202.1 30.3 %collective-permute-start.30 = (bf16[2,4,96,1024]{3,2,1,0:T(8,128)(2,1)}, bf16[2,4,96,1024]{3,2,1,0:T(8,128)(2,1)}, u32[]{:S(2)}, u32[]{:S(2)}) collective-permute-start(bf16[2,4,96,1024]{3,2,1,0:T(8,128)(2,1)} %get-tuple-element.346), channel_id=1, source_target_pairs={{0,1},{1,0},{2,6},{3,7},{4,5},{5,4},{6,2},{7,3},{8,9},{9,8},{10,14... | collective-permute-start | bytes 4718600 | tf_op jit(solution)/shard_map/ppermute | solution.py:56
  218.4 14.0 %collective-permute-start.33 = (bf16[1024,640]{1,0:T(8,128)(2,1)S(1)}, bf16[1024,640]{1,0:T(8,128)(2,1)S(1)}, u32[]{:S(2)}, u32[]{:S(2)}) collective-permute-start(bf16[1024,640]{1,0:T(8,128)(2,1)S(1)} %copy-done.11), channel_id=1, source_target_pairs={{0,2},{1,3},{2,0},{3,1},{4,6},{5,7},{6,4},{7,5},{8,10},{9,11},{10,... | collective-permute-start | bytes 3932168 | tf_op jit(solution)/shard_map/ppermute | solution.py:56
  218.5 13.9 %collective-permute-start.32 = (bf16[4,96,768]{2,1,0:T(8,128)(2,1)S(1)}, bf16[4,96,768]{2,1,0:T(8,128)(2,1)S(1)}, u32[]{:S(2)}, u32[]{:S(2)}) collective-permute-start(bf16[4,96,768]{2,1,0:T(8,128)(2,1)S(1)} %dynamic-slice_bitcast_fusion.1), channel_id=1, source_target_pairs={{0,4},{1,5},{2,3},{3,2},{4,0},{5,1},{6,7},{7,6},{8,12},{9,13},{10,... | collective-permute-start | bytes 1769480 | tf_op jit(solution)/shard_map/ppermute | solution.py:56
  233.2 5.0 %copy-start.10 = (bf16[1024,640]{1,0:T(8,128)(2,1)}, bf16[1024,640]{1,0:T(8,128)(2,1)S(1)}, u32[]{:S(2)}) copy-start(bf16[1024,640]{1,0:T(8,128)(2,1)S(1)} %collective-permute-done.33.refs_3_) | copy-start | bytes 3932164
  233.2 6.0 %collective-permute-start.34 = (bf16[1024,640]{1,0:T(8,128)(2,1)}, bf16[1024,640]{1,0:T(8,128)(2,1)}, u32[]{:S(2)}, u32[]{:S(2)}) collective-permute-start(bf16[1024,640]{1,0:T(8,128)(2,1)} %get-tuple-element.396.vo_ref), channel_id=1, source_target_pairs={{0,2},{1,3},{2,0},{3,1},{4,6},{5,7},{6,4},{7,5},{8,10},{9,11},{10,... | collective-permute-start | bytes 3932168 | tf_op jit(solution)/shard_map/ppermute | solution.py:56
  239.2 17.1 %collective-permute-start.35 = (bf16[4,96,1024]{2,1,0:T(8,128)(2,1)}, bf16[4,96,1024]{2,1,0:T(8,128)(2,1)S(1)}, u32[]{:S(2)}, u32[]{:S(2)}) collective-permute-start(bf16[4,96,1024]{2,1,0:T(8,128)(2,1)} %dynamic-slice_bitcast_fusion), channel_id=1, source_target_pairs={{0,4},{1,5},{2,3},{3,2},{4,0},{5,1},{6,7},{7,6},{8,12},{9,13},{10,... | collective-permute-start | bytes 2359304 | tf_op jit(solution)/shard_map/ppermute | solution.py:56
  240.3 15.9 %collective-permute-start.36 = (bf16[96,768]{1,0:T(8,128)(2,1)}, bf16[96,768]{1,0:T(8,128)(2,1)S(1)}, u32[]{:S(2)}, u32[]{:S(2)}) collective-permute-start(bf16[96,768]{1,0:T(8,128)(2,1)} %get-tuple-element.389), channel_id=1, source_target_pairs={{0,24},{1,25},{2,26},{3,27},{4,28},{5,29},{6,30},{7,31},{8,0},{9,1... | collective-permute-start | bytes 442376 | tf_op jit(solution)/shard_map/ppermute | solution.py:56
  242.7 13.6 %collective-permute-start.37 = (bf16[96,768]{1,0:T(8,128)(2,1)}, bf16[96,768]{1,0:T(8,128)(2,1)S(1)}, u32[]{:S(2)}, u32[]{:S(2)}) collective-permute-start(bf16[96,768]{1,0:T(8,128)(2,1)} %get-tuple-element.390), channel_id=1, source_target_pairs={{0,16},{1,17},{2,18},{3,19},{4,20},{5,21},{6,22},{7,23},{8,24},{9,... | collective-permute-start | bytes 442376 | tf_op jit(solution)/shard_map/ppermute | solution.py:56
  243.1 13.3 %collective-permute-start.38 = (bf16[96,768]{1,0:T(8,128)(2,1)}, bf16[96,768]{1,0:T(8,128)(2,1)S(1)}, u32[]{:S(2)}, u32[]{:S(2)}) collective-permute-start(bf16[96,768]{1,0:T(8,128)(2,1)} %get-tuple-element.391), channel_id=1, source_target_pairs={{0,8},{1,9},{2,10},{3,11},{4,12},{5,13},{6,14},{7,15},{8,16},{9,17... | collective-permute-start | bytes 442376 | tf_op jit(solution)/shard_map/ppermute | solution.py:56
  256.4 16.5 %collective-permute-start.39 = (bf16[2,4,96,640]{3,2,1,0:T(8,128)(2,1)}, bf16[2,4,96,640]{3,2,1,0:T(8,128)(2,1)S(1)}, u32[]{:S(2)}, u32[]{:S(2)}) collective-permute-start(bf16[2,4,96,640]{3,2,1,0:T(8,128)(2,1)} %get-tuple-element.393), channel_id=1, source_target_pairs={{0,1},{1,0},{2,6},{3,7},{4,5},{5,4},{6,2},{7,3},{8,9},{9,8},{10,14... | collective-permute-start | bytes 2949128 | tf_op jit(solution)/shard_map/ppermute | solution.py:56
  257.5 15.3 %collective-permute-start.49 = (f32[48,768]{1,0:T(8,128)S(1)}, f32[48,768]{1,0:T(8,128)S(1)}, u32[]{:S(2)}, u32[]{:S(2)}) collective-permute-start(f32[48,768]{1,0:T(8,128)S(1)} %dynamic-slice_bitcast_fusion.9), channel_id=1, source_target_pairs={{0,2},{1,3},{2,0},{3,1},{4,6},{5,7},{6,4},{7,5},{8,10},{9,11},{10,... | collective-permute-start | bytes 442376 | tf_op jit(solution)/shard_map/ppermute | solution.py:56
  258.0 14.9 %collective-permute-start.40 = (bf16[96,1024]{1,0:T(8,128)(2,1)S(1)}, bf16[96,1024]{1,0:T(8,128)(2,1)S(1)}, u32[]{:S(2)}, u32[]{:S(2)}) collective-permute-start(bf16[96,1024]{1,0:T(8,128)(2,1)S(1)} %get-tuple-element.436), channel_id=1, source_target_pairs={{0,24},{1,25},{2,26},{3,27},{4,28},{5,29},{6,30},{7,31},{8,0},{9,1... | collective-permute-start | bytes 589832 | tf_op jit(solution)/shard_map/ppermute | solution.py:56
  261.6 11.3 %collective-permute-start.41 = (bf16[96,1024]{1,0:T(8,128)(2,1)S(1)}, bf16[96,1024]{1,0:T(8,128)(2,1)S(1)}, u32[]{:S(2)}, u32[]{:S(2)}) collective-permute-start(bf16[96,1024]{1,0:T(8,128)(2,1)S(1)} %get-tuple-element.435), channel_id=1, source_target_pairs={{0,8},{1,9},{2,10},{3,11},{4,12},{5,13},{6,14},{7,15},{8,16},{9,17... | collective-permute-start | bytes 589832 | tf_op jit(solution)/shard_map/ppermute | solution.py:56
  261.6 11.3 %copy-start.14 = (bf16[2,4,96,640]{3,2,1,0:T(8,128)(2,1)S(1)}, bf16[2,4,96,640]{3,2,1,0:T(8,128)(2,1)}, u32[]{:S(2)}) copy-start(bf16[2,4,96,640]{3,2,1,0:T(8,128)(2,1)} %get-tuple-element.399) | copy-start | bytes 2949124
  261.6 18.7 %collective-permute-start.43 = (bf16[96,1024]{1,0:T(8,128)(2,1)S(1)}, bf16[96,1024]{1,0:T(8,128)(2,1)S(1)}, u32[]{:S(2)}, u32[]{:S(2)}) collective-permute-start(bf16[96,1024]{1,0:T(8,128)(2,1)S(1)} %get-tuple-element.434), channel_id=1, source_target_pairs={{0,16},{1,17},{2,18},{3,19},{4,20},{5,21},{6,22},{7,23},{8,24},{9,... | collective-permute-start | bytes 589832 | tf_op jit(solution)/shard_map/ppermute | solution.py:56
  273.2 8.9 %collective-permute-start.42 = (bf16[4,96,640]{2,1,0:T(8,128)(2,1)S(1)}, bf16[4,96,640]{2,1,0:T(8,128)(2,1)S(1)}, u32[]{:S(2)}, u32[]{:S(2)}) collective-permute-start(bf16[4,96,640]{2,1,0:T(8,128)(2,1)S(1)} %dynamic-slice_bitcast_fusion.4), channel_id=1, source_target_pairs={{0,4},{1,5},{2,3},{3,2},{4,0},{5,1},{6,7},{7,6},{8,12},{9,13},{10,... | collective-permute-start | bytes 1474568 | tf_op jit(solution)/shard_map/ppermute | solution.py:56
  280.5 1.5 collective-permute-start.44
  282.3 7.4 %collective-permute-start.45 = (bf16[96,640]{1,0:T(8,128)(2,1)S(1)}, bf16[96,640]{1,0:T(8,128)(2,1)S(1)}, u32[]{:S(2)}, u32[]{:S(2)}) collective-permute-start(bf16[96,640]{1,0:T(8,128)(2,1)S(1)} %get-tuple-element.442), channel_id=1, source_target_pairs={{0,24},{1,25},{2,26},{3,27},{4,28},{5,29},{6,30},{7,31},{8,0},{9,1... | collective-permute-start | bytes 368648 | tf_op jit(solution)/shard_map/ppermute | solution.py:56
  285.5 12.1 %collective-permute-start.46 = (bf16[96,640]{1,0:T(8,128)(2,1)S(1)}, bf16[96,640]{1,0:T(8,128)(2,1)S(1)}, u32[]{:S(2)}, u32[]{:S(2)}) collective-permute-start(bf16[96,640]{1,0:T(8,128)(2,1)S(1)} %get-tuple-element.444), channel_id=1, source_target_pairs={{0,16},{1,17},{2,18},{3,19},{4,20},{5,21},{6,22},{7,23},{8,24},{9,... | collective-permute-start | bytes 368648 | tf_op jit(solution)/shard_map/ppermute | solution.py:56
  288.0 9.6 %collective-permute-start.47 = (bf16[96,640]{1,0:T(8,128)(2,1)S(1)}, bf16[96,640]{1,0:T(8,128)(2,1)S(1)}, u32[]{:S(2)}, u32[]{:S(2)}) collective-permute-start(bf16[96,640]{1,0:T(8,128)(2,1)S(1)} %get-tuple-element.443), channel_id=1, source_target_pairs={{0,8},{1,9},{2,10},{3,11},{4,12},{5,13},{6,14},{7,15},{8,16},{9,17... | collective-permute-start | bytes 368648 | tf_op jit(solution)/shard_map/ppermute | solution.py:56
  297.7 1.5 collective-permute-start.48
  (9 other events, 11.3 us)
